TPU v7x, 256 devices: a whole 4x4x8 slice. The times are simulated.
256 devices in a mesh: tm: 8 (over z_hi, core), space: 32 (over y, x, z_lo).
Axes of the slice: x: 4, y: 4, z: 8 (z_hi: 4, z_lo: 2; z = z_hi * 2 + z_lo), core: 2. Of those that a mesh axis runs over, the one named last changes fastest.
Arguments:
- pressure: float32 [8, 2, 8, 512, 2048], P('tm', None, None, 'space'), may hold values from -6 to 6
- mobility: float32 [8, 2, 8, 512, 2048], P('tm', None, None, 'space'), may hold values from 0.05 to 1
- capacity: float32 [8, 2, 8, 512, 2048], P('tm', None, None, 'space'), may hold values from 0.5 to 2
- misfit_weight: float32 [8, 8, 512, 2048], P('tm', None, 'space'), may hold values from 0.2 to 1
- log_permeability: float32 [512, 2048], P('space'), may hold values from -3 to 3
- direction: float32 [512, 2048], P('space'), may hold values from -9 to 9
Outputs:
- hessian_product: float32 [512, 2048], P('space')
- curvature: float32 [], replicated
All inputs are finite; a program needn't handle non-finite values.
Results may differ from a plain program's by a relative error of at most 0.00002.
Values sent between devices are 32-bit elements; how exact they have to be, the bound alone decides.
A program may use at most 64 MiB of HBM per device.

v0:
```python
import jax
import jax.numpy as jnp
from jax import lax
from jax.sharding import PartitionSpec as P

LAYERS = 8
STEPS = 2


def extended(cells, sides, width):
    for axis, dim in sides:
        count = lax.axis_size(axis)
        ends = count - 1
        head = lax.slice_in_dim(cells, 0, width, axis=dim)
        tail = lax.slice_in_dim(cells, cells.shape[dim] - width, cells.shape[dim], axis=dim)
        cells = jnp.concatenate(
            [
                lax.ppermute(tail, axis, [(i, (i + 1) % count) for i in range(ends)]),
                cells,
                lax.ppermute(head, axis, [((i + 1) % count, i) for i in range(ends)]),
            ],
            axis=dim,
        )
    return cells


def shards(pressure, mobility, capacity, misfit_weight, log_permeability, direction):
    position = lax.axis_index("space")
    devices = lax.axis_size("space")
    height = pressure.shape[3]
    conduct = jnp.exp(log_permeability)
    scaled = conduct * direction
    pressure_w = pressure[0]
    mobility_w = mobility[0]
    capacity_w = capacity[0]
    weight_w = misfit_weight[0]
    face_y = (
        0.5
        * (mobility_w[..., 1:] + mobility_w[..., :-1])
        * (pressure_w[..., 1:] - pressure_w[..., :-1])
    )
    flux_y = 0.5 * (scaled[:, 1:] + scaled[:, :-1]) * face_y
    padded_y = jnp.pad(flux_y, ((0, 0), (0, 0), (0, 0), (1, 1)))
    change_y = padded_y[..., 1:] - padded_y[..., :-1]
    stacked = jnp.stack((pressure_w, mobility_w))
    padded = extended(stacked, (("space", 3),), 1)
    face_x = (
        0.5
        * (padded[1, ..., 1:, :] + padded[1, ..., :-1, :])
        * (padded[0, ..., 1:, :] - padded[0, ..., :-1, :])
    )
    face_index = lax.iota(jnp.int32, height + 1)
    keep_face = ((face_index > 0) | (position > 0)) & (
        (face_index < height) | (position < devices - 1)
    )
    face_x = face_x * keep_face.astype(jnp.float32)[:, None]
    scaled_ext = extended(scaled, (("space", 0),), 1)
    flux_x = 0.5 * (scaled_ext[1:] + scaled_ext[:-1]) * face_x
    change = flux_x[..., 1:, :] - flux_x[..., :-1, :] + change_y
    tangent = change / capacity_w
    adjoint = weight_w * tangent / capacity_w
    adjoint_ext = extended(adjoint, (("space", 2),), 1)
    term_x = face_x * (adjoint_ext[..., :-1, :] - adjoint_ext[..., 1:, :])
    summed_x = jnp.sum(term_x, axis=(0, 1))
    column_x = summed_x[1:] + summed_x[:-1]
    term_y = face_y * (adjoint[..., :-1] - adjoint[..., 1:])
    padded_ty = jnp.pad(term_y, ((0, 0), (0, 0), (0, 0), (1, 1)))
    column_y = jnp.sum(padded_ty[..., 1:] + padded_ty[..., :-1], axis=(0, 1))
    windows = lax.axis_size("tm")
    share = 0.5 * conduct * (column_x + column_y) / (LAYERS * STEPS * windows)
    hessian_product = lax.psum(share, "tm")
    cells = height * devices * direction.shape[1]
    curvature = lax.psum(jnp.sum(direction * hessian_product), "space") / cells
    return (hessian_product, curvature)


def solution(mesh):
    placed = (
        P("tm", None, None, "space", None),
        P("tm", None, None, "space", None),
        P("tm", None, None, "space", None),
        P("tm", None, "space", None),
        P("space", None),
        P("space", None),
    )
    return jax.shard_map(
        shards, mesh=mesh, in_specs=placed, out_specs=(P("space", None), P()), check_vma=False
    )
```

profile of v0, /device:TPU:0, one launch (start us, length us, event | category | flops | bytes accessed | tf_op | source)
XLA Modules:
  0.0 224.2 jit_solution(5592595358356381332)
XLA Ops:
  7.2 1.1 exponential_multiply_fusion
  8.4 1.3 collective-permute-start.2
  9.7 4.5 %collective-permute-start.3 = (f32[1,2048]{1,0:T(1,128)S(1)}, f32[1,2048]{1,0:T(1,128)S(1)}, u32[]{:S(2)}, u32[]{:S(2)}) collective-permute-start(f32[1,2048]{1,0:T(1,128)S(1)} %get-tuple-element.10), channel_id=1, source_target_pairs={{0,1},{1,2},{2,3},{3,4},{4,5},{5,6},{6,7},{7,8},{8,9},{9,10},{10,1... | collective-permute-start | bytes 24584 | tf_op jit(solution)/shard_map/ppermute | solution.py:18
  14.2 1.7 constant_dynamic-update-slice_fusion.1
  16.0 0.2 constant_dynamic-update-slice_fusion
  16.2 1.9 copy-done.2
  18.2 0.4 fusion.27
  18.6 1.3 collective-permute-start
  19.9 4.6 %collective-permute-start.1 = (f32[2,2,8,1,2048]{4,3,2,1,0:T(1,128)S(1)}, f32[2,2,8,1,2048]{4,3,2,1,0:T(1,128)S(1)}, u32[]{:S(2)}, u32[]{:S(2)}) collective-permute-start(f32[2,2,8,1,2048]{4,3,2,1,0:T(1,128)S(1)} %get-tuple-element.7), channel_id=1, source_target_pairs={{0,1},{1,2},{2,3},{3,4},{4,5},{5,6},{6,7},{7,8},{8,9},{9,10},{10,1... | collective-permute-start | bytes 786440 | tf_op jit(solution)/shard_map/ppermute | solution.py:18
  24.6 3.5 %broadcast_multiply_fusion.1 = (f32[2,8,16,2047]{3,2,1,0:T(8,128)S(1)}, f32[2,8,16,2047]{3,2,1,0:T(8,128)S(1)}) fusion(f32[16,2047]{1,0:T(8,128)S(1)} %fusion.24, f32[2,8,16,2048]{3,2,1,0:T(8,128)S(1)} %bitcast.10, f32[2,8,16,2048]{3,2,1,0:T(8,128)} %bitcast.11), kind=kLoop, calls=%fused_computation.36 | loop fusion | flops 2620160 | bytes 12707776 | tf_op jit(solution)/shard_map/mul | solution.py:42
  28.3 0.4 collective-permute-done
  28.6 1.6 broadcast_multiply_fusion
  30.2 1.1 fusion.14
  31.6 5.8 %collective-permute-start.4 = (f32[2,8,1,2048]{3,2,1,0:T(1,128)S(1)}, f32[2,8,1,2048]{3,2,1,0:T(1,128)S(1)}, u32[]{:S(2)}, u32[]{:S(2)}) collective-permute-start(f32[2,8,1,2048]{3,2,1,0:T(1,128)S(1)} %get-tuple-element.9), channel_id=1, source_target_pairs={{0,1},{1,2},{2,3},{3,4},{4,5},{5,6},{6,7},{7,8},{8,9},{9,10},{10,1... | collective-permute-start | bytes 393224 | tf_op jit(solution)/shard_map/ppermute | solution.py:18
  37.3 1.3 collective-permute-start.5
  38.6 0.8 fusion.17
  39.4 0.6 fusion.16
  40.1 6.2 %collective-permute-done.5 = f32[2,8,1,2048]{3,2,1,0:T(1,128)S(1)} collective-permute-done((f32[2,8,1,2048]{3,2,1,0:T(1,128)S(1)}, f32[2,8,1,2048]{3,2,1,0:T(1,128)S(1)}, u32[]{:S(2)}, u32[]{:S(2)}) %collective-permute-start.5) | collective-permute-done | bytes 131104 | tf_op jit(solution)/shard_map/ppermute | solution.py:20
  46.2 0.8 fusion.9
  47.1 0.7 fusion.23
  47.9 81.8 %all-reduce.4.cloned.1.call-done = f32[16,2048]{1,0:T(8,128)} async-done(((f32[16,2048]{1,0:T(8,128)}), f32[16,2048]{1,0:T(8,128)}) %all-reduce.4.cloned.1.call-update) | async-done | bytes 131088 | tf_op jit(solution)/shard_map/psum | solution.py:71
  129.7 1.5 multiply_reduce_fusion
  131.2 82.8 %psum.15 = f32[]{:T(128)} all-reduce(f32[]{:T(128)} %multiply_reduce_fusion), channel_id=1, replica_groups=mesh['tm'=8,'space'=32] {'space'}, use_global_device_ids=true, to_apply=%region_4.5 | all-reduce | flops 1 | bytes 8 | tf_op jit(solution)/shard_map/psum | solution.py:73
  214.7 1.6 copy.10
  (26 shorter events, 0.6 us)
Async XLA Ops:
  7.2 122.5 %all-reduce.4.cloned.1.call-start = ((), (), s32[]{:S(2)}) async-start(), calls=%async_computation | async-start | bytes 262144 | tf_op jit(solution)/shard_map/psum | solution.py:71
  7.2 8.8 %copy-start.1 = (f32[1,2,8,16,2048]{4,3,2,1,0:T(8,128)S(1)}, f32[1,2,8,16,2048]{4,3,2,1,0:T(8,128)}, u32[]{:S(2)}) copy-start(f32[1,2,8,16,2048]{4,3,2,1,0:T(8,128)} %param.7) | copy-start | bytes 6291460
  8.4 19.8 %collective-permute-start.2 = (f32[1,2048]{1,0:T(1,128)S(1)}, f32[1,2048]{1,0:T(1,128)S(1)}, u32[]{:S(2)}, u32[]{:S(2)}) collective-permute-start(f32[1,2048]{1,0:T(1,128)S(1)} %get-tuple-element.11), channel_id=1, source_target_pairs={{1,0},{2,1},{3,2},{4,3},{5,4},{6,5},{7,6},{8,7},{9,8},{10,9},{11,1... | collective-permute-start | bytes 24584 | tf_op jit(solution)/shard_map/ppermute | solution.py:20
  9.7 18.5 %collective-permute-start.3 = (f32[1,2048]{1,0:T(1,128)S(1)}, f32[1,2048]{1,0:T(1,128)S(1)}, u32[]{:S(2)}, u32[]{:S(2)}) collective-permute-start(f32[1,2048]{1,0:T(1,128)S(1)} %get-tuple-element.10), channel_id=1, source_target_pairs={{0,1},{1,2},{2,3},{3,4},{4,5},{5,6},{6,7},{7,8},{8,9},{9,10},{10,1... | collective-permute-start | bytes 24584 | tf_op jit(solution)/shard_map/ppermute | solution.py:18
  16.0 8.6 %copy-start = (f32[1,2,8,16,2048]{4,3,2,1,0:T(8,128)S(1)}, f32[1,2,8,16,2048]{4,3,2,1,0:T(8,128)}, u32[]{:S(2)}) copy-start(f32[1,2,8,16,2048]{4,3,2,1,0:T(8,128)} %param.6) | copy-start | bytes 6291460
  16.2 1.9 copy-start.2
  18.6 10.0 %collective-permute-start = (f32[2,2,8,1,2048]{4,3,2,1,0:T(1,128)S(1)}, f32[2,2,8,1,2048]{4,3,2,1,0:T(1,128)S(1)}, u32[]{:S(2)}, u32[]{:S(2)}) collective-permute-start(f32[2,2,8,1,2048]{4,3,2,1,0:T(1,128)S(1)} %get-tuple-element.6), channel_id=1, source_target_pairs={{1,0},{2,1},{3,2},{4,3},{5,4},{6,5},{7,6},{8,7},{9,8},{10,9},{11,1... | collective-permute-start | bytes 786440 | tf_op jit(solution)/shard_map/ppermute | solution.py:20
  19.9 8.7 %collective-permute-start.1 = (f32[2,2,8,1,2048]{4,3,2,1,0:T(1,128)S(1)}, f32[2,2,8,1,2048]{4,3,2,1,0:T(1,128)S(1)}, u32[]{:S(2)}, u32[]{:S(2)}) collective-permute-start(f32[2,2,8,1,2048]{4,3,2,1,0:T(1,128)S(1)} %get-tuple-element.7), channel_id=1, source_target_pairs={{0,1},{1,2},{2,3},{3,4},{4,5},{5,6},{6,7},{7,8},{8,9},{9,10},{10,1... | collective-permute-start | bytes 786440 | tf_op jit(solution)/shard_map/ppermute | solution.py:18
  24.6 4.0 %copy-start.3 = (f32[2,2,8,16,2048]{4,3,2,1,0:T(8,128)S(1)}, f32[2,2,8,16,2048]{4,3,2,1,0:T(8,128)}, u32[]{:S(2)}) copy-start(f32[2,2,8,16,2048]{4,3,2,1,0:T(8,128)} %copy-done.2) | copy-start | bytes 12582916
  28.2 2.0 copy-start.4
  28.2 2.0 copy-start.5
  31.6 8.5 %collective-permute-start.4 = (f32[2,8,1,2048]{3,2,1,0:T(1,128)S(1)}, f32[2,8,1,2048]{3,2,1,0:T(1,128)S(1)}, u32[]{:S(2)}, u32[]{:S(2)}) collective-permute-start(f32[2,8,1,2048]{3,2,1,0:T(1,128)S(1)} %get-tuple-element.9), channel_id=1, source_target_pairs={{0,1},{1,2},{2,3},{3,4},{4,5},{5,6},{6,7},{7,8},{8,9},{9,10},{10,1... | collective-permute-start | bytes 393224 | tf_op jit(solution)/shard_map/ppermute | solution.py:18
  37.3 8.9 %collective-permute-start.5 = (f32[2,8,1,2048]{3,2,1,0:T(1,128)S(1)}, f32[2,8,1,2048]{3,2,1,0:T(1,128)S(1)}, u32[]{:S(2)}, u32[]{:S(2)}) collective-permute-start(f32[2,8,1,2048]{3,2,1,0:T(1,128)S(1)} %get-tuple-element.8), channel_id=1, source_target_pairs={{1,0},{2,1},{3,2},{4,3},{5,4},{6,5},{7,6},{8,7},{9,8},{10,9},{11,1... | collective-permute-start | bytes 393224 | tf_op jit(solution)/shard_map/ppermute | solution.py:20
  46.2 0.9 copy-start.6
  46.2 83.5 %copy-start.7 = (f32[16,2048]{1,0:T(8,128)S(1)}, f32[16,2048]{1,0:T(8,128)}, u32[]{:S(2)}) copy-start(f32[16,2048]{1,0:T(8,128)} %param.11) | copy-start | bytes 393220
Sparse Core Ops, SparseCore 0:
  48.0 81.6 all-reduce.3
where the time goes:
time: 225 us; the launch traced here: 224 us
  waiting for transfers between devices  88.4 us (39%)
  blocking collectives  82.8 us (37%)
  starting transfers between devices  18.8 us (8%)
  between operations  16.1 us (7%)
  other arithmetic  12 us (5%)
  local copies, waits for them, and re-layouts  6.22 us (3%)
    psum x1, blocking collectives, shards(): curvature = lax.psum(jnp.sum(direction * hessian_product), 'space') / cells  82.8 us
    psum x1, waiting for transfers between devices, shards(): hessian_product = lax.psum(share, 'tm')  81.8 us
    ppermute x3, starting transfers between devices, extended(): lax.ppermute(tail, axis, [(i, (i + 1) % count) for i in range(ends)])  14.9 us
    ppermute x3, waiting for transfers between devices, extended(): lax.ppermute(head, axis, [((i + 1) % count, i) for i in range(ends)])  6.54 us
    unnamed x18, local copies, waits for them, and re-layouts  5.38 us
  transfers between devices with their start and end apart: 7, of which 3 were waited for; matrix products, arithmetic and copies ran while one was open for 3% of the time, Pallas kernels for 0%

commit v1 on v0

v1 whole, which is shorter than its diff:
```python
import functools

import jax
import jax.numpy as jnp
from jax import lax
from jax.experimental import pallas as pl
from jax.experimental.pallas import tpu as pltpu
from jax.sharding import PartitionSpec as P

LANES = 128
SUBLANES = 8
CHIPS_X = 4
CORES = 2
Z_LO = 2
MESH = pl.DeviceIdType.MESH
F32 = jnp.float32


def kernel(
    dims,
    p_hbm,
    m_hbm,
    c_hbm,
    w_hbm,
    lp_hbm,
    d_hbm,
    out,
    cur,
    pv,
    mv,
    cv,
    wv,
    lpv,
    dv,
    pm,
    fx,
    adj,
    txa,
    tyc,
    sbx,
    sby,
    sce,
    rce,
    gsend,
    grecv,
    tot,
    rec,
    part,
    rsb,
    agb,
    sx,
    sz,
    sy,
    local_sem,
    send_sem,
    recv_sem,
):
    tms, spaces, steps, layers, rows, width = dims
    tiles = width // LANES
    zhs = tms // CORES
    ys = spaces // (CHIPS_X * Z_LO)
    zs = zhs * Z_LO
    quarter = tiles // zhs
    last = rows

    tm = lax.axis_index("tm")
    sp = lax.axis_index("space")
    zh, core = tm // CORES, tm % CORES
    zl = sp % Z_LO
    x = (sp // Z_LO) % CHIPS_X
    y = sp // (Z_LO * CHIPS_X)
    z = zh * Z_LO + zl
    left = (sp + spaces - 1) % spaces
    right = (sp + 1) % spaces
    other = (tm + 1) - 2 * core

    per = layers * rows

    def tile_loads(src, dst, first, count, sem):
        def one(j, carry):
            pltpu.make_async_copy(
                src.at[pl.ds(first, count), pl.ds(pl.multiple_of(j * LANES, LANES), LANES)],
                dst.at[j],
                sem,
            ).start()
            return carry

        lax.fori_loop(0, tiles, one, 0)

    def await_tiles(dst, sem):
        pltpu.make_async_copy(dst, dst, sem).wait()

    for s in range(steps):
        tile_loads(p_hbm, pv.at[s], s * per, per, local_sem.at[s])
        tile_loads(m_hbm, mv.at[s], s * per, per, local_sem.at[steps + s])
    load_lp = pltpu.make_async_copy(lp_hbm, lpv, local_sem.at[2 * steps])
    load_d = pltpu.make_async_copy(d_hbm, dv, local_sem.at[2 * steps + 1])
    load_lp.start()
    load_d.start()

    x_group = CORES * CHIPS_X
    my_x = core * CHIPS_X + x

    def x_peer(k):
        index = (my_x + k) % x_group
        return (zh * CORES + index // CHIPS_X, sp + (index % CHIPS_X - x) * Z_LO)

    def z_peer(k):
        to = (z + k) % zs
        return ((to // Z_LO) * CORES + core, sp - zl + to % Z_LO)

    def y_peer(k):
        to = (y + k) % ys
        return (tm, sp + (to - y) * CHIPS_X * Z_LO)

    def tm_peer(k, c):
        return (((zh + k) % zhs) * CORES + (core + c) % CORES, sp)

    greet = [(zh * CORES + c, side) for side in (left, right) for c in range(CORES)]
    greet += [tm_peer(k, c) for k in range(zhs) for c in range(CORES) if (k, c) != (0, 0)]
    greet += [z_peer(k) for k in range(1, zs)]
    greet += [x_peer(k) for k in range(1, x_group)]
    greet += [y_peer(k) for k in range(1, ys)]
    barrier = pltpu.get_barrier_semaphore()
    for peer in greet:
        pl.semaphore_signal(barrier, inc=1, device_id=peer, device_id_type=MESH)

    tile_loads(c_hbm, cv, 0, steps * per, local_sem.at[2 * steps + 2])
    tile_loads(w_hbm, wv, 0, per, local_sem.at[2 * steps + 3])

    sem_count = [0]
    started = []

    def send(src, dst, device, send_index, recv_index):
        copy = pltpu.make_async_remote_copy(
            src_ref=src,
            dst_ref=dst,
            send_sem=send_sem.at[send_index],
            recv_sem=recv_sem.at[recv_index],
            device_id=device,
            device_id_type=MESH,
        )
        copy.start()
        started.append(copy)

    def arrived(dst, recv_index):
        pltpu.make_async_copy(dst, dst, recv_sem.at[recv_index]).wait()

    def take(n):
        first = sem_count[0]
        sem_count[0] += n
        return first

    def transposed(ref, base, i):
        return [ref[j, pl.ds(base + i, layers, stride=rows), :] for j in range(tiles)]

    def spread(s, i):
        for which, ref in enumerate((pv, mv)):
            for j, tile in enumerate(transposed(ref.at[s], 0, i)):
                pm[i + 1, s, which, :, j * LANES : (j + 1) * LANES] = tile

    halo = take(2 * steps)
    for s in range(steps):
        await_tiles(pv.at[s], local_sem.at[s])
        await_tiles(mv.at[s], local_sem.at[steps + s])
        spread(s, 0)
        spread(s, rows - 1)
        if s == 0:
            pl.semaphore_wait(barrier, len(greet))
        send(pm.at[1, s], pm.at[last + 1, s], (tm, left), halo + 2 * s, halo + 2 * s)
        send(pm.at[last, s], pm.at[0, s], (tm, right), halo + 2 * s + 1, halo + 2 * s + 1)

    load_lp.wait()
    load_d.wait()
    scaled = jnp.exp(lpv[...]) * dv[...]
    sce[0] = scaled[0:1, :]
    sce[1] = scaled[rows - 1 : rows, :]
    edge = take(2)
    send(sce.at[0], rce.at[1], (tm, left), edge, edge)
    send(sce.at[1], rce.at[0], (tm, right), edge + 1, edge + 1)

    wide = (layers, width)
    for i in range(rows):
        row = scaled[i : i + 1, :]
        if i + 1 < rows:
            sbx[i + 1] = jnp.broadcast_to(0.25 * (row + scaled[i + 1 : i + 2, :]), wide)
        sby[i] = jnp.broadcast_to(0.25 * (row + pltpu.roll(row, width - 1, 1)), wide)

    def spread_inner(i, carry):
        for s in range(steps):
            spread(s, i)
        return carry

    lax.fori_loop(1, rows - 1, spread_inner, 0)

    lane = lax.broadcasted_iota(jnp.int32, (layers, LANES), 1)
    not_last = lane < LANES - 1
    not_first = lane > 0

    def cut(j):
        return slice(j * LANES, (j + 1) * LANES)

    def face_x(f, carry):
        for s in range(steps):
            for j in range(tiles):
                c = cut(j)
                fx[f, s, :, c] = (pm[f, s, 1, :, c] + pm[f + 1, s, 1, :, c]) * (
                    pm[f + 1, s, 0, :, c] - pm[f, s, 0, :, c]
                )
        return carry

    def cell_row(r, curvature):
        i = r - 1

        def one_step(s):
            held = {}

            def once(name, j, make):
                if (name, j) not in held:
                    held[name, j] = make()
                return held[name, j]

            def pressure(j):
                return once("p", j, lambda: pm[r, s, 0, :, cut(j)])

            def mobility(j):
                return once("m", j, lambda: pm[r, s, 1, :, cut(j)])

            def back(name, get, j):
                return once("b" + name, j, lambda: pltpu.roll(get(j), LANES - 1, 1))

            def ahead(name, get, j):
                after = back(name, get, j + 1) if j + 1 < tiles else get(j)
                return jnp.where(not_last, back(name, get, j), after)

            def before(name, get, j):
                here = once("f" + name, j, lambda: pltpu.roll(get(j), 1, 1))
                if j == 0:
                    return jnp.where(not_first, here, 0.0)
                return jnp.where(not_first, here, held["f" + name, j - 1])

            def face_y(j):
                return once(
                    "fy",
                    j,
                    lambda: (mobility(j) + ahead("m", mobility, j))
                    * (ahead("p", pressure, j) - pressure(j)),
                )

            def flux_y(j):
                return once("gy", j, lambda: face_y(j) * sby[i, :, cut(j)])

            def change(j):
                c = cut(j)
                return once(
                    "ch",
                    j,
                    lambda: fx[r, s, :, c] * sbx[r, :, c]
                    - fx[r - 1, s, :, c] * sbx[r - 1, :, c]
                    + (flux_y(j) - before("gy", flux_y, j)),
                )

            def adjoint(j):
                def make():
                    cap = cv[j, pl.ds(s * per + i, layers, stride=rows), :]
                    weight = wv[j, pl.ds(i, layers, stride=rows), :]
                    value = weight * change(j) / (cap * cap)
                    adj[r, s, :, cut(j)] = value
                    return value

                return once("a", j, make)

            def term_y(j):
                return once(
                    "ty", j, lambda: face_y(j) * (adjoint(j) - ahead("a", adjoint, j))
                )

            return change, adjoint, lambda j: term_y(j) + before("ty", term_y, j)

        parts = [one_step(s) for s in range(steps)]
        for j in range(tiles):
            total = None
            for change, adjoint, both in parts:
                value = both(j)
                total = value if total is None else total + value
                curvature = curvature + adjoint(j) * change(j)
            tyc[i, :, cut(j)] = total
        return curvature

    def face_terms(f, low=True, high=True):
        for j in range(tiles):
            c = cut(j)
            total = None
            for s in range(steps):
                if low and high:
                    difference = adj[f, s, :, c] - adj[f + 1, s, :, c]
                elif low:
                    difference = adj[f, s, :, c]
                else:
                    difference = -adj[f + 1, s, :, c]
                value = fx[f, s, :, c] * difference
                total = value if total is None else total + value
            txa[f, :, c] = total

    def total_row(i):
        for j in range(tiles):
            c = cut(j)
            value = txa[i, :, c] + txa[i + 1, :, c] + tyc[i, :, c]
            tot[j, pl.ds(i, 1), :] = jnp.sum(value, axis=0, keepdims=True)

    lax.fori_loop(1, rows, face_x, 0)
    await_tiles(cv, local_sem.at[2 * steps + 2])
    await_tiles(wv, local_sem.at[2 * steps + 3])
    curvature = lax.fori_loop(2, rows, cell_row, jnp.zeros((layers, LANES), F32))

    def inner_faces(f, carry):
        face_terms(f)
        return carry

    lax.fori_loop(2, rows - 1, inner_faces, 0)

    def inner_rows(i, carry):
        total_row(i)
        return carry

    lax.fori_loop(2, rows - 2, inner_rows, 0)

    arrived(rce.at[0], edge + 1)
    arrived(rce.at[1], edge)
    sbx[0] = jnp.broadcast_to(0.25 * (rce[0] + scaled[0:1, :]), wide)
    sbx[last] = jnp.broadcast_to(0.25 * (rce[1] + scaled[rows - 1 : rows, :]), wide)
    for s in range(steps):
        arrived(pm.at[last + 1, s], halo + 2 * s)
        arrived(pm.at[0, s], halo + 2 * s + 1)

    @pl.when(sp == 0)
    def _():
        pm[0] = pm[1]

    @pl.when(sp == spaces - 1)
    def _():
        pm[last + 1] = pm[last]

    lax.fori_loop(0, 2, lambda k, carry: face_x(k * last, carry), 0)
    curvature = lax.fori_loop(0, 2, lambda k, carry: cell_row(1 + k * (rows - 1), carry), curvature)
    face_terms(0, low=False)
    face_terms(last, high=False)
    face_terms(1)
    face_terms(rows - 1)
    for j in range(tiles):
        gsend[0, :, cut(j)] = jnp.sum(txa[0, :, cut(j)], axis=0, keepdims=True)
        gsend[1, :, cut(j)] = jnp.sum(txa[last, :, cut(j)], axis=0, keepdims=True)
    for i in (0, 1, rows - 2, rows - 1):
        total_row(i)

    half = rows // CORES
    pair = take(1)
    ghost = take(2)
    ghost_in = take(2)
    send(
        tot.at[:, pl.ds(pl.multiple_of((1 - core) * half, half), half), :],
        rec,
        (other, sp),
        pair,
        pair,
    )
    send(gsend.at[0], grecv.at[core], (zh * CORES + 1, left), ghost, ghost_in + core)
    send(gsend.at[1], grecv.at[core], (zh * CORES, right), ghost + 1, ghost_in + core)

    sx[my_x] = jnp.sum(curvature, axis=0, keepdims=True)
    over_x = take(x_group)
    for k in range(1, x_group):
        send(sx.at[my_x], sx.at[my_x], x_peer(k), over_x + k, over_x + k)

    arrived(grecv.at[0], ghost_in)
    arrived(grecv.at[1], ghost_in + 1)
    sub = lax.broadcasted_iota(jnp.int32, (half, LANES), 0)
    here = sub == core * (half - 1)
    for j in range(tiles):
        c = cut(j)
        mine = tot[j, pl.ds(pl.multiple_of(core * half, half), half), :]
        part[j] = mine + jnp.where(here, grecv[0, :, c] + grecv[1, :, c], 0.0)
    arrived(rec, pair)
    part[...] = part[...] + rec[...]

    scatter = take(zhs)

    def columns(q):
        return pl.ds(q * quarter, quarter)

    for k in range(1, zhs):
        to = (zh + k) % zhs
        send(part.at[columns(to)], rsb.at[k], tm_peer(k, 0), scatter + k, scatter + k)

    for k in range(1, x_group):
        arrived(sx.at[(my_x + x_group - k) % x_group], over_x + k)
    sz[z] = jnp.sum(sx[...], axis=0)
    over_z = take(zs)
    for k in range(1, zs):
        send(sz.at[z], sz.at[z], z_peer(k), over_z + k, over_z + k)

    reduced = part[columns(zh)]
    for k in range(1, zhs):
        arrived(rsb.at[k], scatter + k)
        reduced = reduced + rsb[k]
    agb[core, zh] = reduced
    gather = take(tms)
    for k in range(zhs):
        for c in range(CORES):
            if (k, c) != (0, 0):
                index = gather + k * CORES + c
                send(agb.at[core, zh], agb.at[core, zh], tm_peer(k, c), index, index)

    for k in range(1, zs):
        arrived(sz.at[(z + zs - k) % zs], over_z + k)
    sy[y] = jnp.sum(sz[...], axis=0)
    over_y = take(ys)
    for k in range(1, ys):
        send(sy.at[y], sy.at[y], y_peer(k), over_y + k, over_y + k)

    for k in range(zhs):
        for c in range(CORES):
            if (k, c) != (0, 0):
                source = agb.at[(core + c) % CORES, (zh + zhs - k) % zhs]
                arrived(source, gather + k * CORES + c)
    for c in range(CORES):
        for q in range(zhs):
            for j in range(quarter):
                out[c * half : (c + 1) * half, cut(q * quarter + j)] = agb[c, q, j]

    for k in range(1, ys):
        arrived(sy.at[(y + ys - k) % ys], over_y + k)
    whole = jnp.sum(sy[...], axis=0)
    scale = 1.0 / (layers * steps * tms * rows * spaces * width)
    cur[...] = jnp.broadcast_to(jnp.sum(whole, axis=1, keepdims=True) * scale, cur.shape)

    for copy in started:
        copy.wait_send()


def shards(tms, spaces, pressure, mobility, capacity, misfit_weight, log_permeability, direction):
    _, steps, layers, rows, width = pressure.shape
    dims = (tms, spaces, steps, layers, rows, width)
    tiles = width // LANES
    zhs = tms // CORES
    ys = spaces // (CHIPS_X * Z_LO)
    zs = zhs * Z_LO
    x_group = CORES * CHIPS_X
    per = layers * rows
    half = rows // CORES
    copies = 2 * steps + 2 + 1 + 4 + x_group + zhs + zs + tms + ys
    vmem = pltpu.VMEM
    total, curvature = pl.pallas_call(
        functools.partial(kernel, dims),
        out_shape=(
            jax.ShapeDtypeStruct((rows, width), F32),
            jax.ShapeDtypeStruct((1, LANES), F32),
        ),
        in_specs=[pl.BlockSpec(memory_space=pl.ANY)] * 6,
        out_specs=(
            pl.BlockSpec(memory_space=pltpu.VMEM),
            pl.BlockSpec(memory_space=pltpu.VMEM),
        ),
        scratch_shapes=[
            vmem((steps, tiles, per, LANES), F32),
            vmem((steps, tiles, per, LANES), F32),
            vmem((tiles, steps * per, LANES), F32),
            vmem((tiles, per, LANES), F32),
            vmem((rows, width), F32),
            vmem((rows, width), F32),
            vmem((rows + 2, steps, 2, layers, width), F32),
            vmem((rows + 1, steps, layers, width), F32),
            vmem((rows + 2, steps, layers, width), F32),
            vmem((rows + 1, layers, width), F32),
            vmem((rows, layers, width), F32),
            vmem((rows + 1, layers, width), F32),
            vmem((rows, layers, width), F32),
            vmem((2, 1, width), F32),
            vmem((2, 1, width), F32),
            vmem((2, 1, width), F32),
            vmem((2, 1, width), F32),
            vmem((tiles, rows, LANES), F32),
            vmem((tiles, half, LANES), F32),
            vmem((tiles, half, LANES), F32),
            vmem((zhs, tiles // zhs, half, LANES), F32),
            vmem((CORES, zhs, tiles // zhs, half, LANES), F32),
            vmem((x_group, 1, LANES), F32),
            vmem((zs, 1, LANES), F32),
            vmem((ys, 1, LANES), F32),
            pltpu.SemaphoreType.DMA((2 * steps + 4,)),
            pltpu.SemaphoreType.DMA((copies,)),
            pltpu.SemaphoreType.DMA((copies,)),
        ],
        compiler_params=pltpu.CompilerParams(
            collective_id=0, has_side_effects=True, vmem_limit_bytes=56 << 20
        ),
        cost_estimate=pl.CostEstimate(
            flops=50 * steps * per * width,
            bytes_accessed=4 * (7 * steps * per * width // 2),
            transcendentals=rows * width,
        ),
    )(
        pressure.reshape(steps * per, width),
        mobility.reshape(steps * per, width),
        capacity.reshape(steps * per, width),
        misfit_weight.reshape(per, width),
        log_permeability,
        direction,
    )
    factor = 0.25 / (layers * steps * tms)
    return jnp.exp(log_permeability) * total * factor, curvature[0, 0]


def solution(mesh):
    placed = (
        P("tm", None, None, "space", None),
        P("tm", None, None, "space", None),
        P("tm", None, None, "space", None),
        P("tm", None, "space", None),
        P("space", None),
        P("space", None),
    )
    return jax.shard_map(
        functools.partial(shards, mesh.shape["tm"], mesh.shape["space"]),
        mesh=mesh,
        in_specs=placed,
        out_specs=(P("space", None), P()),
        check_vma=False,
    )
```

time: 225 us -> 47.6 us (0.21)
  the two profiles are of different devices: /device:TPU:0 before, /device:TPU:1 now
where the time goes in v1:
time: 47.6 us; the launch traced here: 47.5 us
  Pallas kernels  43.5 us (91%)
  between operations  2.41 us (5%)
  other arithmetic  1.59 us (3%)
    pallas_call x1, Pallas kernels, shards(): pl.pallas_call(functools.partial(kernel, dims), out_shape=(jax.ShapeDtype...  43.5 us
    mul x1, other arithmetic, shards(): return (jnp.exp(log_permeability) * total * factor, curvature[0, 0])  1.59 us

profile of v1, /device:TPU:1, one launch (start us, length us, event | category | flops | bytes accessed | tf_op | source)
XLA Modules:
  0.0 47.5 jit_solution(12755942283462902683)
XLA Ops:
  0.6 0.0 copy-start
  0.6 43.5 %shard_map.77 = (f32[16,2048]{1,0:T(8,128)}, f32[1,128]{1,0:T(1,128)}) custom-call(f32[256,2048]{1,0:T(8,128)} %bitcast.6, f32[256,2048]{1,0:T(8,128)} %bitcast.7, f32[256,2048]{1,0:T(8,128)} %bitcast.8, f32[128,2048]{1,0:T(8,128)} %bitcast.9, f32[16,2048]{1,0:T(8,128)} %lp_hbm.1, f32[16,2048]{1,0:T(8,128)} %d_hbm.1), custom_call_target="tpu_custom_call" | custom-call | flops 26214400 | bytes 7340032 | tf_op jit(solution)/shard_map/pallas_call | solution.py:453
  44.2 0.0 copy-done
  44.2 1.6 %multiply_multiply_fusion = f32[16,2048]{1,0:T(8,128)} fusion(f32[16,2048]{1,0:T(8,128)} %get-tuple-element.4, f32[16,2048]{1,0:T(8,128)S(1)} %copy-done), kind=kLoop, calls=%fused_computation | loop fusion | flops 65536 | bytes 393216 | tf_op jit(solution)/shard_map/mul | solution.py:511
Async XLA Ops:
  0.6 43.5 %copy-start = (f32[16,2048]{1,0:T(8,128)S(1)}, f32[16,2048]{1,0:T(8,128)}, u32[]{:S(2)}) copy-start(f32[16,2048]{1,0:T(8,128)} %lp_hbm.1) | copy-start | bytes 393220

commit v2 on v1

v2 whole, which is shorter than its diff:
```python
import functools

import jax
import jax.numpy as jnp
from jax import lax
from jax.experimental import pallas as pl
from jax.experimental.pallas import tpu as pltpu
from jax.sharding import PartitionSpec as P

LANES = 128
SUBLANES = 8
CHIPS_X = 4
CORES = 2
Z_LO = 2
MESH = pl.DeviceIdType.MESH
F32 = jnp.float32


def kernel(
    dims,
    p_hbm,
    m_hbm,
    c_hbm,
    w_hbm,
    lp_hbm,
    d_hbm,
    out,
    cur,
    pv,
    mv,
    cv,
    wv,
    lpv,
    dv,
    pm,
    fx,
    adj,
    txa,
    tyc,
    sbx,
    sby,
    sce,
    rce,
    inner,
    inner_in,
    inner_sum,
    rsb,
    agb,
    edges,
    edges_in,
    edge_z,
    ghost_z,
    final,
    sz,
    sxy,
    local_sem,
    send_sem,
    recv_sem,
):
    tms, spaces, steps, layers, rows, width = dims
    tiles = width // LANES
    zhs = tms // CORES
    ys = spaces // (CHIPS_X * Z_LO)
    zs = zhs * Z_LO
    last = rows
    row_tiles = tiles // SUBLANES
    row_blocks = rows // SUBLANES
    layer_rows = row_blocks * tiles * SUBLANES
    state_rows = layers * layer_rows

    tm = lax.axis_index("tm")
    sp = lax.axis_index("space")
    zh, core = tm // CORES, tm % CORES
    zl = sp % Z_LO
    x = (sp // Z_LO) % CHIPS_X
    y = sp // (Z_LO * CHIPS_X)
    z = zh * Z_LO + zl
    left = (sp + spaces - 1) % spaces
    right = (sp + 1) % spaces
    other = (tm + 1) - 2 * core

    loads = {}

    def load(name, src, dst, index):
        loads[name] = pltpu.make_async_copy(src, dst, local_sem.at[index])
        loads[name].start()

    for s in range(steps):
        part = pl.ds(s * state_rows, state_rows)
        load(("p", s), p_hbm.at[part, :], pv.at[part, :], 2 * s)
        load(("m", s), m_hbm.at[part, :], mv.at[part, :], 2 * s + 1)
    load("lp", lp_hbm, lpv, 2 * steps)
    load("d", d_hbm, dv, 2 * steps + 1)

    line = zs * CORES
    my_line = z * CORES + core
    plane = ys * CHIPS_X
    my_plane = y * CHIPS_X + x

    def line_peer(k):
        index = (my_line + k) % line
        to = index // CORES
        return ((to // Z_LO) * CORES + index % CORES, sp - zl + to % Z_LO)

    def plane_peer(k):
        return (tm, ((my_plane + k) % plane) * Z_LO + zl)

    def z_peer(k):
        return (((zh + k) % zhs) * CORES + core, sp)

    greet = [(t, side) for side in (left, right) for t in range(tms)]
    greet += [((tm + k) % tms, sp) for k in range(1, tms)]
    greet += [plane_peer(k) for k in range(1, plane)]
    barrier = pltpu.get_barrier_semaphore()
    for peer in greet:
        pl.semaphore_signal(barrier, inc=1, device_id=peer, device_id_type=MESH)

    sem_count = [0]
    started = []

    def send(src, dst, device, send_index, recv_index):
        copy = pltpu.make_async_remote_copy(
            src_ref=src,
            dst_ref=dst,
            send_sem=send_sem.at[send_index],
            recv_sem=recv_sem.at[recv_index],
            device_id=device,
            device_id_type=MESH,
        )
        copy.start()
        started.append(copy)

    def arrived(dst, recv_index):
        pltpu.make_async_copy(dst, dst, recv_sem.at[recv_index]).wait()

    def take(n):
        first = sem_count[0]
        sem_count[0] += n
        return first

    def layers_of(ref, s, i, j):
        first = (
            s * state_rows + (i // SUBLANES) * (tiles * SUBLANES) + j * SUBLANES + i % SUBLANES
        )
        return ref[pl.ds(first, layers, stride=layer_rows), :]

    def cut(j):
        return slice(j * LANES, (j + 1) * LANES)

    def spread(s, i):
        for which, ref in enumerate((pv, mv)):
            for j in range(tiles):
                pm[i + 1, s, which, :, cut(j)] = layers_of(ref, s, i, j)

    halo = take(2 * steps)
    for s in range(steps):
        loads["p", s].wait()
        loads["m", s].wait()
        spread(s, 0)
        spread(s, rows - 1)
        if s == 0:
            pl.semaphore_wait(barrier, len(greet))
        send(pm.at[1, s], pm.at[last + 1, s], (tm, left), halo + 2 * s, halo + 2 * s)
        send(pm.at[last, s], pm.at[0, s], (tm, right), halo + 2 * s + 1, halo + 2 * s + 1)
    load("c", c_hbm, cv, 2 * steps + 2)
    load("w", w_hbm, wv, 2 * steps + 3)

    loads["lp"].wait()
    loads["d"].wait()
    scaled = jnp.exp(lpv[...]) * dv[...]
    sce[0] = scaled[0:1, :]
    sce[1] = scaled[rows - 1 : rows, :]
    edge = take(2)
    send(sce.at[0], rce.at[1], (tm, left), edge, edge)
    send(sce.at[1], rce.at[0], (tm, right), edge + 1, edge + 1)

    wide = (layers, width)
    for i in range(rows):
        row = scaled[i : i + 1, :]
        if i + 1 < rows:
            sbx[i + 1] = jnp.broadcast_to(0.25 * (row + scaled[i + 1 : i + 2, :]), wide)
        sby[i] = jnp.broadcast_to(0.25 * (row + pltpu.roll(row, width - 1, 1)), wide)

    def spread_inner(i, carry):
        for s in range(steps):
            spread(s, i)
        return carry

    lax.fori_loop(1, rows - 1, spread_inner, 0)

    lane = lax.broadcasted_iota(jnp.int32, (layers, LANES), 1)
    not_last = lane < LANES - 1
    not_first = lane > 0

    def face_x(f, carry):
        for s in range(steps):
            for j in range(tiles):
                c = cut(j)
                fx[f, s, :, c] = (pm[f, s, 1, :, c] + pm[f + 1, s, 1, :, c]) * (
                    pm[f + 1, s, 0, :, c] - pm[f, s, 0, :, c]
                )
        return carry

    def cell_row(r, curvature):
        i = r - 1

        def one_step(s):
            held = {}

            def once(name, j, make):
                if (name, j) not in held:
                    held[name, j] = make()
                return held[name, j]

            def pressure(j):
                return once("p", j, lambda: pm[r, s, 0, :, cut(j)])

            def mobility(j):
                return once("m", j, lambda: pm[r, s, 1, :, cut(j)])

            def back(name, get, j):
                return once("b" + name, j, lambda: pltpu.roll(get(j), LANES - 1, 1))

            def ahead(name, get, j):
                after = back(name, get, j + 1) if j + 1 < tiles else get(j)
                return jnp.where(not_last, back(name, get, j), after)

            def before(name, get, j):
                here = once("f" + name, j, lambda: pltpu.roll(get(j), 1, 1))
                if j == 0:
                    return jnp.where(not_first, here, 0.0)
                return jnp.where(not_first, here, held["f" + name, j - 1])

            def face_y(j):
                return once(
                    "fy",
                    j,
                    lambda: (mobility(j) + ahead("m", mobility, j))
                    * (ahead("p", pressure, j) - pressure(j)),
                )

            def flux_y(j):
                return once("gy", j, lambda: face_y(j) * sby[i, :, cut(j)])

            def change(j):
                c = cut(j)
                return once(
                    "ch",
                    j,
                    lambda: fx[r, s, :, c] * sbx[r, :, c]
                    - fx[r - 1, s, :, c] * sbx[r - 1, :, c]
                    + (flux_y(j) - before("gy", flux_y, j)),
                )

            def adjoint(j):
                def make():
                    cap = layers_of(cv, s, i, j)
                    weight = layers_of(wv, 0, i, j)
                    square = cap * cap
                    inverse = pl.reciprocal(square, approx=True)
                    inverse = inverse * (2.0 - square * inverse)
                    value = weight * change(j) * inverse
                    adj[r, s, :, cut(j)] = value
                    return value

                return once("a", j, make)

            def term_y(j):
                return once(
                    "ty", j, lambda: face_y(j) * (adjoint(j) - ahead("a", adjoint, j))
                )

            return change, adjoint, lambda j: term_y(j) + before("ty", term_y, j)

        parts = [one_step(s) for s in range(steps)]
        for j in range(tiles):
            total = None
            for change, adjoint, both in parts:
                value = both(j)
                total = value if total is None else total + value
                curvature = curvature + adjoint(j) * change(j)
            tyc[i, :, cut(j)] = total
        return curvature

    def face_terms(f, low=True, high=True):
        for j in range(tiles):
            c = cut(j)
            total = None
            for s in range(steps):
                if low and high:
                    difference = adj[f, s, :, c] - adj[f + 1, s, :, c]
                elif low:
                    difference = adj[f, s, :, c]
                else:
                    difference = -adj[f + 1, s, :, c]
                value = fx[f, s, :, c] * difference
                total = value if total is None else total + value
            txa[f, :, c] = total

    def pack(dst, first, j, value):
        tile = first + j // SUBLANES
        low = j % SUBLANES
        dst[tile, low : low + 1, :] = jnp.sum(value, axis=0, keepdims=True)

    def pack_total(dst, first, i):
        for j in range(tiles):
            c = cut(j)
            pack(dst, first, j, txa[i, :, c] + txa[i + 1, :, c] + tyc[i, :, c])

    lax.fori_loop(1, rows, face_x, 0)
    loads["c"].wait()
    loads["w"].wait()
    curvature = lax.fori_loop(2, rows, cell_row, jnp.zeros((layers, LANES), F32))

    def inner_faces(f, carry):
        face_terms(f)
        return carry

    lax.fori_loop(2, rows - 1, inner_faces, 0)

    def inner_rows(i, carry):
        pack_total(inner, (i - 2) * row_tiles, i)
        return carry

    lax.fori_loop(2, rows - 2, inner_rows, 0)

    half_tiles = (rows // CORES - 2) * row_tiles
    chunk = half_tiles // zhs
    inner_pair = take(1)
    send(
        inner.at[pl.ds((1 - core) * half_tiles, half_tiles)],
        inner_in,
        (other, sp),
        inner_pair,
        inner_pair,
    )
    arrived(inner_in, inner_pair)
    inner_sum[...] = inner[pl.ds(core * half_tiles, half_tiles)] + inner_in[...]
    scatter = take(zhs)
    for k in range(1, zhs):
        to = (zh + k) % zhs
        send(
            inner_sum.at[pl.ds(to * chunk, chunk)],
            rsb.at[k],
            z_peer(k),
            scatter + k,
            scatter + k,
        )

    arrived(rce.at[0], edge + 1)
    arrived(rce.at[1], edge)
    sbx[0] = jnp.broadcast_to(0.25 * (rce[0] + scaled[0:1, :]), wide)
    sbx[last] = jnp.broadcast_to(0.25 * (rce[1] + scaled[rows - 1 : rows, :]), wide)
    for s in range(steps):
        arrived(pm.at[last + 1, s], halo + 2 * s)
        arrived(pm.at[0, s], halo + 2 * s + 1)

    @pl.when(sp == 0)
    def _():
        pm[0] = pm[1]

    @pl.when(sp == spaces - 1)
    def _():
        pm[last + 1] = pm[last]

    lax.fori_loop(0, 2, lambda k, carry: face_x(k * last, carry), 0)
    curvature = lax.fori_loop(0, 2, lambda k, carry: cell_row(1 + k * (rows - 1), carry), curvature)

    sz[my_line] = jnp.sum(curvature, axis=0, keepdims=True)
    over_line = take(line)
    for k in range(1, line):
        send(sz.at[my_line], sz.at[my_line], line_peer(k), over_line + k, over_line + k)

    face_terms(0, low=False)
    face_terms(last, high=False)
    face_terms(1)
    face_terms(rows - 1)
    for c, (edge_row, inner_row, face) in enumerate(((0, 1, 0), (rows - 1, rows - 2, last))):
        pack_total(edges.at[c], 0, edge_row)
        pack_total(edges.at[c], row_tiles, inner_row)
        for j in range(tiles):
            pack(edges.at[c], 2 * row_tiles, j, txa[face, :, cut(j)])
    edge_pair = take(1)
    send(edges.at[1 - core], edges_in, (other, sp), edge_pair, edge_pair)

    reduced = inner_sum[pl.ds(zh * chunk, chunk)]
    for k in range(1, zhs):
        arrived(rsb.at[k], scatter + k)
        reduced = reduced + rsb[k]
    agb[core, pl.ds(zh * chunk, chunk)] = reduced
    mine = agb.at[core, pl.ds(zh * chunk, chunk)]
    gather = take(zhs)
    forward = take(zhs)
    for k in range(1, zhs):
        send(mine, mine, z_peer(k), gather + k, gather + k)
    send(mine, mine, (other, sp), forward, forward)

    two = 2 * row_tiles
    arrived(edges_in, edge_pair)
    summed = edges[core] + edges_in[...]
    edge_z[zh] = summed
    over_z = take(zhs)
    ghost = take(zhs)
    for k in range(1, zhs):
        send(
            edge_z.at[zh, pl.ds(0, two)],
            edge_z.at[zh, pl.ds(0, two)],
            z_peer(k),
            over_z + k,
            over_z + k,
        )
    side = left + core * (right - left)
    for k in range(zhs):
        send(
            edge_z.at[zh, pl.ds(two, row_tiles)],
            ghost_z.at[zh],
            (((zh + k) % zhs) * CORES + 1 - core, side),
            ghost + k,
            ghost + k,
        )

    for k in range(1, line):
        arrived(sz.at[(my_line + line - k) % line], over_line + k)
    sxy[my_plane] = jnp.sum(sz[...], axis=0)
    over_plane = take(plane)
    for k in range(1, plane):
        send(sxy.at[my_plane], sxy.at[my_plane], plane_peer(k), over_plane + k, over_plane + k)

    def unpack(src, first, i):
        for j in range(tiles):
            low = j % SUBLANES
            out[i : i + 1, cut(j)] = src[first + j // SUBLANES, low : low + 1, :]

    for k in range(1, zhs):
        whose = agb.at[core, pl.ds(((zh + zhs - k) % zhs) * chunk, chunk)]
        arrived(whose, gather + k)
        send(whose, whose, (other, sp), forward + k, forward + k)

    for k in range(1, zhs):
        arrived(edge_z.at[(zh + zhs - k) % zhs, pl.ds(0, two)], over_z + k)
    for k in range(zhs):
        arrived(ghost_z.at[(zh + zhs - k) % zhs], ghost + k)
    total = edge_z[0, 0:two]
    beyond = ghost_z[0]
    for k in range(1, zhs):
        total = total + edge_z[k, 0:two]
        beyond = beyond + ghost_z[k]
    final[core, pl.ds(0, row_tiles)] = total[:row_tiles] + beyond
    final[core, pl.ds(row_tiles, row_tiles)] = total[row_tiles:]
    final_pair = take(1)
    send(final.at[core], final.at[core], (other, sp), final_pair, final_pair)

    for k in range(zhs):
        whose = agb.at[1 - core, pl.ds(((zh + zhs - k) % zhs) * chunk, chunk)]
        arrived(whose, forward + k)
    for i in range(2, rows - 2):
        first = (i - 2) * row_tiles
        unpack(agb.at[first // half_tiles], first % half_tiles, i)
    arrived(final.at[1 - core], final_pair)
    for c, (edge_row, inner_row) in enumerate(((0, 1), (rows - 1, rows - 2))):
        unpack(final.at[c], 0, edge_row)
        unpack(final.at[c], row_tiles, inner_row)

    for k in range(1, plane):
        arrived(sxy.at[(my_plane + plane - k) % plane], over_plane + k)
    whole = jnp.sum(sxy[...], axis=0)
    scale = 1.0 / (layers * steps * tms * rows * spaces * width)
    cur[...] = jnp.broadcast_to(jnp.sum(whole, axis=1, keepdims=True) * scale, cur.shape)

    for copy in started:
        copy.wait_send()


def shards(tms, spaces, pressure, mobility, capacity, misfit_weight, log_permeability, direction):
    _, steps, layers, rows, width = pressure.shape
    dims = (tms, spaces, steps, layers, rows, width)
    tiles = width // LANES
    zhs = tms // CORES
    ys = spaces // (CHIPS_X * Z_LO)
    line = zhs * Z_LO * CORES
    plane = ys * CHIPS_X
    flat = layers * rows * tiles
    row_tiles = tiles // SUBLANES
    half_tiles = (rows // CORES - 2) * row_tiles
    chunk = half_tiles // zhs
    copies = 2 * steps + 2 + 3 + 5 * zhs + line + plane
    vmem = pltpu.VMEM

    def in_tiles(array):
        count = array.size // (SUBLANES * width)
        cut = array.reshape(count, SUBLANES, tiles, LANES).transpose(0, 2, 1, 3)
        return cut.reshape(count * tiles * SUBLANES, LANES)

    def block(*shape):
        return vmem((*shape, SUBLANES, LANES), F32)

    total, curvature = pl.pallas_call(
        functools.partial(kernel, dims),
        out_shape=(
            jax.ShapeDtypeStruct((rows, width), F32),
            jax.ShapeDtypeStruct((1, LANES), F32),
        ),
        in_specs=[pl.BlockSpec(memory_space=pl.ANY)] * 6,
        out_specs=(
            pl.BlockSpec(memory_space=pltpu.VMEM),
            pl.BlockSpec(memory_space=pltpu.VMEM),
        ),
        scratch_shapes=[
            vmem((steps * flat, LANES), F32),
            vmem((steps * flat, LANES), F32),
            vmem((steps * flat, LANES), F32),
            vmem((flat, LANES), F32),
            vmem((rows, width), F32),
            vmem((rows, width), F32),
            vmem((rows + 2, steps, 2, layers, width), F32),
            vmem((rows + 1, steps, layers, width), F32),
            vmem((rows + 2, steps, layers, width), F32),
            vmem((rows + 1, layers, width), F32),
            vmem((rows, layers, width), F32),
            vmem((rows + 1, layers, width), F32),
            vmem((rows, layers, width), F32),
            vmem((2, 1, width), F32),
            vmem((2, 1, width), F32),
            block(CORES * half_tiles),
            block(half_tiles),
            block(half_tiles),
            block(zhs, chunk),
            block(CORES, half_tiles),
            block(CORES, 3 * row_tiles),
            block(3 * row_tiles),
            block(zhs, 3 * row_tiles),
            block(zhs, row_tiles),
            block(CORES, 2 * row_tiles),
            vmem((line, 1, LANES), F32),
            vmem((plane, 1, LANES), F32),
            pltpu.SemaphoreType.DMA((2 * steps + 4,)),
            pltpu.SemaphoreType.DMA((copies,)),
            pltpu.SemaphoreType.DMA((copies,)),
        ],
        compiler_params=pltpu.CompilerParams(
            collective_id=0, has_side_effects=True, vmem_limit_bytes=56 << 20
        ),
        cost_estimate=pl.CostEstimate(
            flops=50 * steps * flat * LANES,
            bytes_accessed=14 * steps * flat * LANES,
            transcendentals=rows * width,
        ),
    )(
        in_tiles(pressure),
        in_tiles(mobility),
        in_tiles(capacity),
        in_tiles(misfit_weight),
        log_permeability,
        direction,
    )
    factor = 0.25 / (layers * steps * tms)
    return jnp.exp(log_permeability) * total * factor, curvature[0, 0]


def solution(mesh):
    placed = (
        P("tm", None, None, "space", None),
        P("tm", None, None, "space", None),
        P("tm", None, None, "space", None),
        P("tm", None, "space", None),
        P("space", None),
        P("space", None),
    )
    return jax.shard_map(
        functools.partial(shards, mesh.shape["tm"], mesh.shape["space"]),
        mesh=mesh,
        in_specs=placed,
        out_specs=(P("space", None), P()),
        check_vma=False,
    )
```

time: 47.6 us -> 44.5 us (0.935)
  Pallas kernels: 43.5 us -> 40.4 us
    pallas_call x1, Pallas kernels: 43.5 us -> 40.4 us  [shards(): pl.pallas_call(functools.partial(kernel, dims), out_shape=(jax.ShapeDtype...]
where the time goes in v2:
time: 44.5 us; the launch traced here: 44.4 us
  Pallas kernels  40.4 us (91%)
  between operations  2.41 us (5%)
  other arithmetic  1.59 us (4%)
    pallas_call x1, Pallas kernels, shards(): pl.pallas_call(functools.partial(kernel, dims), out_shape=(jax.ShapeDtype...  40.4 us
    mul x1, other arithmetic, shards(): return (jnp.exp(log_permeability) * total * factor, curvature[0, 0])  1.59 us

profile of v2, /device:TPU:1, one launch (start us, length us, event | category | flops | bytes accessed | tf_op | source)
XLA Modules:
  0.0 44.4 jit_solution(3835955333073074495)
XLA Ops:
  0.6 0.0 copy-start
  0.6 40.4 %shard_map.77 = (f32[16,2048]{1,0:T(8,128)}, f32[1,128]{1,0:T(1,128)}) custom-call(f32[4096,128]{1,0:T(8,128)} %bitcast.22, f32[4096,128]{1,0:T(8,128)} %bitcast.23, f32[4096,128]{1,0:T(8,128)} %bitcast.24, f32[2048,128]{1,0:T(8,128)} %bitcast.25, f32[16,2048]{1,0:T(8,128)} %lp_hbm.1, f32[16,2048]{1,0:T(8,128)} %d_hbm.1), custom_call_target="tpu_custom_call" | custom-call | flops 26214400 | bytes 7340032 | tf_op jit(solution)/shard_map/pallas_call | solution.py:497
  41.1 0.0 copy-done
  41.1 1.6 %multiply_multiply_fusion = f32[16,2048]{1,0:T(8,128)} fusion(f32[16,2048]{1,0:T(8,128)} %get-tuple-element.4, f32[16,2048]{1,0:T(8,128)S(1)} %copy-done), kind=kLoop, calls=%fused_computation | loop fusion | flops 65536 | bytes 393216 | tf_op jit(solution)/shard_map/mul | solution.py:557
Async XLA Ops:
  0.6 40.4 %copy-start = (f32[16,2048]{1,0:T(8,128)S(1)}, f32[16,2048]{1,0:T(8,128)}, u32[]{:S(2)}) copy-start(f32[16,2048]{1,0:T(8,128)} %lp_hbm.1) | copy-start | bytes 393220

commit v3 on v2

--- a/solution.py
+++ b/solution.py
@@ -36,9 +36,10 @@
     fx,
     adj,
     txa,
-    tyc,
+    ty,
     sbx,
     sby,
+    sbb,
     sce,
     rce,
     inner,
@@ -91,6 +92,8 @@
         load(("m", s), m_hbm.at[part, :], mv.at[part, :], 2 * s + 1)
     load("lp", lp_hbm, lpv, 2 * steps)
     load("d", d_hbm, dv, 2 * steps + 1)
+    load("c", c_hbm, cv, 2 * steps + 2)
+    load("w", w_hbm, wv, 2 * steps + 3)
 
     line = zs * CORES
     my_line = z * CORES + core
@@ -152,6 +155,7 @@
             for j in range(tiles):
                 pm[i + 1, s, which, :, cut(j)] = layers_of(ref, s, i, j)
 
+    near, far = pl.ds(0, width // 2), pl.ds(width // 2, width // 2)
     halo = take(2 * steps)
     for s in range(steps):
         loads["p", s].wait()
@@ -160,10 +164,18 @@
         spread(s, rows - 1)
         if s == 0:
             pl.semaphore_wait(barrier, len(greet))
-        send(pm.at[1, s], pm.at[last + 1, s], (tm, left), halo + 2 * s, halo + 2 * s)
-        send(pm.at[last, s], pm.at[0, s], (tm, right), halo + 2 * s + 1, halo + 2 * s + 1)
-    load("c", c_hbm, cv, 2 * steps + 2)
-    load("w", w_hbm, wv, 2 * steps + 3)
+        to_left, to_right = (far, near) if s == 0 else (pl.ds(0, width), pl.ds(0, width))
+        for row, goal, side, columns, index in (
+            (1, last + 1, left, to_left, halo + 2 * s),
+            (last, 0, right, to_right, halo + 2 * s + 1),
+        ):
+            send(
+                pm.at[row, s, :, :, columns],
+                pm.at[goal, s, :, :, columns],
+                (tm, side),
+                index,
+                index,
+            )
 
     loads["lp"].wait()
     loads["d"].wait()
@@ -180,6 +192,7 @@
         if i + 1 < rows:
             sbx[i + 1] = jnp.broadcast_to(0.25 * (row + scaled[i + 1 : i + 2, :]), wide)
         sby[i] = jnp.broadcast_to(0.25 * (row + pltpu.roll(row, width - 1, 1)), wide)
+        sbb[i] = jnp.broadcast_to(0.25 * (row + pltpu.roll(row, 1, 1)), wide)
 
     def spread_inner(i, carry):
         for s in range(steps):
@@ -192,94 +205,65 @@
     not_last = lane < LANES - 1
     not_first = lane > 0
 
+    def face_part(f, s, part):
+        for j in part:
+            c = cut(j)
+            fx[f, s, :, c] = (pm[f, s, 1, :, c] + pm[f + 1, s, 1, :, c]) * (
+                pm[f + 1, s, 0, :, c] - pm[f, s, 0, :, c]
+            )
+
     def face_x(f, carry):
         for s in range(steps):
-            for j in range(tiles):
-                c = cut(j)
-                fx[f, s, :, c] = (pm[f, s, 1, :, c] + pm[f + 1, s, 1, :, c]) * (
-                    pm[f + 1, s, 0, :, c] - pm[f, s, 0, :, c]
-                )
+            face_part(f, s, range(tiles))
         return carry
 
     def cell_row(r, curvature):
         i = r - 1
 
-        def one_step(s):
-            held = {}
-
-            def once(name, j, make):
-                if (name, j) not in held:
-                    held[name, j] = make()
-                return held[name, j]
-
-            def pressure(j):
-                return once("p", j, lambda: pm[r, s, 0, :, cut(j)])
-
-            def mobility(j):
-                return once("m", j, lambda: pm[r, s, 1, :, cut(j)])
-
-            def back(name, get, j):
-                return once("b" + name, j, lambda: pltpu.roll(get(j), LANES - 1, 1))
-
-            def ahead(name, get, j):
-                after = back(name, get, j + 1) if j + 1 < tiles else get(j)
-                return jnp.where(not_last, back(name, get, j), after)
-
-            def before(name, get, j):
-                here = once("f" + name, j, lambda: pltpu.roll(get(j), 1, 1))
-                if j == 0:
-                    return jnp.where(not_first, here, 0.0)
-                return jnp.where(not_first, here, held["f" + name, j - 1])
-
-            def face_y(j):
-                return once(
-                    "fy",
-                    j,
-                    lambda: (mobility(j) + ahead("m", mobility, j))
-                    * (ahead("p", pressure, j) - pressure(j)),
+        def ahead(here, later):
+            return jnp.where(not_last, here, later)
+
+        def turned(s, j):
+            pressure, mobility = pm[r, s, 0, :, cut(j)], pm[r, s, 1, :, cut(j)]
+            return (
+                pressure,
+                mobility,
+                pltpu.roll(pressure, LANES - 1, 1),
+                pltpu.roll(mobility, LANES - 1, 1),
+            )
+
+        here = [turned(s, 0) for s in range(steps)]
+        spill = [0.0] * steps
+        for j in range(tiles):
+            c = cut(j)
+            low, high = None, None
+            for s in range(steps):
+                pressure, mobility, p_back, m_back = here[s]
+                if j + 1 < tiles:
+                    here[s] = turned(s, j + 1)
+                    p_next, m_next = here[s][2], here[s][3]
+                else:
+                    p_next, m_next = pressure, mobility
+                face = (mobility + ahead(m_back, m_next)) * (ahead(p_back, p_next) - pressure)
+                turned_face = pltpu.roll(face, 1, 1)
+                before = jnp.where(not_first, turned_face, spill[s])
+                spill[s] = turned_face
+                change = (
+                    fx[r, s, :, c] * sbx[r, :, c]
+                    - fx[r - 1, s, :, c] * sbx[r - 1, :, c]
+                    + (face * sby[i, :, c] - before * sbb[i, :, c])
                 )
-
-            def flux_y(j):
-                return once("gy", j, lambda: face_y(j) * sby[i, :, cut(j)])
-
-            def change(j):
-                c = cut(j)
-                return once(
-                    "ch",
-                    j,
-                    lambda: fx[r, s, :, c] * sbx[r, :, c]
-                    - fx[r - 1, s, :, c] * sbx[r - 1, :, c]
-                    + (flux_y(j) - before("gy", flux_y, j)),
-                )
-
-            def adjoint(j):
-                def make():
-                    cap = layers_of(cv, s, i, j)
-                    weight = layers_of(wv, 0, i, j)
-                    square = cap * cap
-                    inverse = pl.reciprocal(square, approx=True)
-                    inverse = inverse * (2.0 - square * inverse)
-                    value = weight * change(j) * inverse
-                    adj[r, s, :, cut(j)] = value
-                    return value
-
-                return once("a", j, make)
-
-            def term_y(j):
-                return once(
-                    "ty", j, lambda: face_y(j) * (adjoint(j) - ahead("a", adjoint, j))
-                )
-
-            return change, adjoint, lambda j: term_y(j) + before("ty", term_y, j)
-
-        parts = [one_step(s) for s in range(steps)]
-        for j in range(tiles):
-            total = None
-            for change, adjoint, both in parts:
-                value = both(j)
-                total = value if total is None else total + value
-                curvature = curvature + adjoint(j) * change(j)
-            tyc[i, :, cut(j)] = total
+                square = layers_of(cv, s, i, j)
+                square = square * square
+                inverse = pl.reciprocal(square, approx=True)
+                inverse = inverse * (2.0 - square * inverse)
+                value = layers_of(wv, 0, i, j) * change * inverse
+                adj[r, s, :, c] = value
+                curvature = curvature + value * change
+                low = face * value if low is None else low + face * value
+                high = before * value if high is None else high + before * value
+            ty[i, 0, :, c] = low
+            ty[i, 1, :, c] = high
         return curvature
 
     def face_terms(f, low=True, high=True):
@@ -297,15 +281,40 @@
                 total = value if total is None else total + value
             txa[f, :, c] = total
 
-    def pack(dst, first, j, value):
-        tile = first + j // SUBLANES
-        low = j % SUBLANES
-        dst[tile, low : low + 1, :] = jnp.sum(value, axis=0, keepdims=True)
+    sub = lax.broadcasted_iota(jnp.int32, (SUBLANES, LANES), 0)
+    below = [(sub // d) % 2 == 0 for d in (1, 2, 4)]
+
+    def fold(values):
+        for bit, d in enumerate((1, 2, 4)):
+            pairs = zip(values[::2], values[1::2])
+            values = [
+                jnp.where(below[bit], a, b) + pltpu.roll(jnp.where(below[bit], b, a), d, 0)
+                for a, b in pairs
+            ]
+        return values[0]
+
+    def folded(get):
+        return [
+            fold([get(cut(g * SUBLANES + k)) for k in range(SUBLANES)]) for g in range(row_tiles)
+        ]
 
     def pack_total(dst, first, i):
-        for j in range(tiles):
-            c = cut(j)
-            pack(dst, first, j, txa[i, :, c] + txa[i + 1, :, c] + tyc[i, :, c])
+        own = folded(
+            lambda c: txa[i, :, c] + txa[i + 1, :, c] + (ty[i, 0, :, c] - ty[i, 1, :, c])
+        )
+        low = [pltpu.roll(v, 1, 1) for v in folded(lambda c: ty[i, 0, :, c])]
+        high = [pltpu.roll(v, LANES - 1, 1) for v in folded(lambda c: ty[i, 1, :, c])]
+        zero = jnp.zeros((SUBLANES, LANES), F32)
+        low_down = [pltpu.roll(v, 1, 0) for v in low]
+        high_up = [pltpu.roll(v, SUBLANES - 1, 0) for v in high]
+        for g in range(row_tiles):
+            prior = low_down[g - 1] if g else zero
+            after = high_up[g + 1] if g + 1 < row_tiles else zero
+            from_low = jnp.where(not_first, low[g], jnp.where(sub > 0, low_down[g], prior))
+            from_high = jnp.where(
+                not_last, high[g], jnp.where(sub < SUBLANES - 1, high_up[g], after)
+            )
+            dst[first + g] = own[g] + from_low - from_high
 
     lax.fori_loop(1, rows, face_x, 0)
     loads["c"].wait()
@@ -334,6 +343,18 @@
         inner_pair,
         inner_pair,
     )
+
+    near_tiles, far_tiles = range(tiles // 2), range(tiles // 2, tiles)
+    product = take(2)
+    arrived(pm.at[0, 0, :, :, near], halo + 1)
+    face_part(0, 0, near_tiles)
+    to_left, to_right = fx.at[0, 0, :, near], fx.at[last, 0, :, far]
+    send(to_left, fx.at[last, 0, :, near], (tm, left), product, product)
+    arrived(pm.at[last + 1, 0, :, :, far], halo)
+    face_part(last, 0, far_tiles)
+    send(to_right, fx.at[0, 0, :, far], (tm, right), product + 1, product + 1)
+    products = [started.pop(), started.pop()]
+
     arrived(inner_in, inner_pair)
     inner_sum[...] = inner[pl.ds(core * half_tiles, half_tiles)] + inner_in[...]
     scatter = take(zhs)
@@ -351,19 +372,25 @@
     arrived(rce.at[1], edge)
     sbx[0] = jnp.broadcast_to(0.25 * (rce[0] + scaled[0:1, :]), wide)
     sbx[last] = jnp.broadcast_to(0.25 * (rce[1] + scaled[rows - 1 : rows, :]), wide)
-    for s in range(steps):
+    for s in range(1, steps):
         arrived(pm.at[last + 1, s], halo + 2 * s)
         arrived(pm.at[0, s], halo + 2 * s + 1)
+        face_part(0, s, range(tiles))
+        face_part(last, s, range(tiles))
+    arrived(fx.at[last, 0, :, near], product)
+    arrived(fx.at[0, 0, :, far], product + 1)
+
+    for copy in products:
+        copy.wait_send()
 
     @pl.when(sp == 0)
     def _():
-        pm[0] = pm[1]
+        fx[0] = jnp.zeros((steps, layers, width), F32)
 
     @pl.when(sp == spaces - 1)
     def _():
-        pm[last + 1] = pm[last]
-
-    lax.fori_loop(0, 2, lambda k, carry: face_x(k * last, carry), 0)
+        fx[last] = jnp.zeros((steps, layers, width), F32)
+
     curvature = lax.fori_loop(0, 2, lambda k, carry: cell_row(1 + k * (rows - 1), carry), curvature)
 
     sz[my_line] = jnp.sum(curvature, axis=0, keepdims=True)
@@ -378,8 +405,8 @@
     for c, (edge_row, inner_row, face) in enumerate(((0, 1, 0), (rows - 1, rows - 2, last))):
         pack_total(edges.at[c], 0, edge_row)
         pack_total(edges.at[c], row_tiles, inner_row)
-        for j in range(tiles):
-            pack(edges.at[c], 2 * row_tiles, j, txa[face, :, cut(j)])
+        for g, value in enumerate(folded(lambda k: txa[face, :, k])):
+            edges[c, 2 * row_tiles + g] = value
     edge_pair = take(1)
     send(edges.at[1 - core], edges_in, (other, sp), edge_pair, edge_pair)
 
@@ -483,7 +510,7 @@
     row_tiles = tiles // SUBLANES
     half_tiles = (rows // CORES - 2) * row_tiles
     chunk = half_tiles // zhs
-    copies = 2 * steps + 2 + 3 + 5 * zhs + line + plane
+    copies = 2 * steps + 4 + 3 + 5 * zhs + line + plane
     vmem = pltpu.VMEM
 
     def in_tiles(array):
@@ -516,8 +543,9 @@
             vmem((rows + 1, steps, layers, width), F32),
             vmem((rows + 2, steps, layers, width), F32),
             vmem((rows + 1, layers, width), F32),
+            vmem((rows, 2, layers, width), F32),
+            vmem((rows + 1, layers, width), F32),
             vmem((rows, layers, width), F32),
-            vmem((rows + 1, layers, width), F32),
             vmem((rows, layers, width), F32),
             vmem((2, 1, width), F32),
             vmem((2, 1, width), F32),

time: 44.5 us -> 42.6 us (0.957)
  Pallas kernels: 40.4 us -> 38.5 us
    pallas_call x1, Pallas kernels: 40.4 us -> 38.5 us  [shards(): pl.pallas_call(functools.partial(kernel, dims), out_shape=(jax.ShapeDtype...]
where the time goes in v3:
time: 42.6 us; the launch traced here: 42.5 us
  Pallas kernels  38.5 us (90%)
  between operations  2.41 us (6%)
  other arithmetic  1.59 us (4%)
    pallas_call x1, Pallas kernels, shards(): pl.pallas_call(functools.partial(kernel, dims), out_shape=(jax.ShapeDtype...  38.5 us
    mul x1, other arithmetic, shards(): return (jnp.exp(log_permeability) * total * factor, curvature[0, 0])  1.59 us

profile of v3, /device:TPU:1, one launch (start us, length us, event | category | flops | bytes accessed | tf_op | source)
XLA Modules:
  0.0 42.5 jit_solution(12475961263028289861)
XLA Ops:
  0.6 0.0 copy-start
  0.6 38.5 %shard_map.77 = (f32[16,2048]{1,0:T(8,128)}, f32[1,128]{1,0:T(1,128)}) custom-call(f32[4096,128]{1,0:T(8,128)} %bitcast.22, f32[4096,128]{1,0:T(8,128)} %bitcast.23, f32[4096,128]{1,0:T(8,128)} %bitcast.24, f32[2048,128]{1,0:T(8,128)} %bitcast.25, f32[16,2048]{1,0:T(8,128)} %lp_hbm.1, f32[16,2048]{1,0:T(8,128)} %d_hbm.1), custom_call_target="tpu_custom_call" | custom-call | flops 26214400 | bytes 7340032 | tf_op jit(solution)/shard_map/pallas_call | solution.py:524
  39.1 0.0 copy-done
  39.1 1.6 %multiply_multiply_fusion = f32[16,2048]{1,0:T(8,128)} fusion(f32[16,2048]{1,0:T(8,128)} %get-tuple-element.4, f32[16,2048]{1,0:T(8,128)S(1)} %copy-done), kind=kLoop, calls=%fused_computation | loop fusion | flops 65536 | bytes 393216 | tf_op jit(solution)/shard_map/mul | solution.py:585
Async XLA Ops:
  0.6 38.5 %copy-start = (f32[16,2048]{1,0:T(8,128)S(1)}, f32[16,2048]{1,0:T(8,128)}, u32[]{:S(2)}) copy-start(f32[16,2048]{1,0:T(8,128)} %lp_hbm.1) | copy-start | bytes 393220

commit v4 on v3

--- a/solution.py
+++ b/solution.py
@@ -40,6 +40,8 @@
     sbx,
     sby,
     sbb,
+    factor,
+    px,
     sce,
     rce,
     inner,
@@ -92,8 +94,6 @@
         load(("m", s), m_hbm.at[part, :], mv.at[part, :], 2 * s + 1)
     load("lp", lp_hbm, lpv, 2 * steps)
     load("d", d_hbm, dv, 2 * steps + 1)
-    load("c", c_hbm, cv, 2 * steps + 2)
-    load("w", w_hbm, wv, 2 * steps + 3)
 
     line = zs * CORES
     my_line = z * CORES + core
@@ -163,6 +163,8 @@
         spread(s, 0)
         spread(s, rows - 1)
         if s == 0:
+            load("c", c_hbm, cv, 2 * steps + 2)
+            load("w", w_hbm, wv, 2 * steps + 3)
             pl.semaphore_wait(barrier, len(greet))
         to_left, to_right = (far, near) if s == 0 else (pl.ds(0, width), pl.ds(0, width))
         for row, goal, side, columns, index in (
@@ -179,7 +181,9 @@
 
     loads["lp"].wait()
     loads["d"].wait()
-    scaled = jnp.exp(lpv[...]) * dv[...]
+    conduct = jnp.exp(lpv[...])
+    factor[...] = conduct * (0.25 / (layers * steps * tms))
+    scaled = conduct * dv[...]
     sce[0] = scaled[0:1, :]
     sce[1] = scaled[rows - 1 : rows, :]
     edge = take(2)
@@ -217,7 +221,7 @@
             face_part(f, s, range(tiles))
         return carry
 
-    def cell_row(r, curvature):
+    def cell_row(r, curvature, states=range(steps), add=False):
         i = r - 1
 
         def ahead(here, later):
@@ -232,12 +236,13 @@
                 pltpu.roll(mobility, LANES - 1, 1),
             )
 
-        here = [turned(s, 0) for s in range(steps)]
-        spill = [0.0] * steps
+        here = {s: turned(s, 0) for s in states}
+        spill = {s: 0.0 for s in states}
         for j in range(tiles):
             c = cut(j)
-            low, high = None, None
-            for s in range(steps):
+            piece = pl.ds(j * SUBLANES, SUBLANES)
+            low, high = (ty[i, 0, piece, :], ty[i, 1, piece, :]) if add else (None, None)
+            for s in states:
                 pressure, mobility, p_back, m_back = here[s]
                 if j + 1 < tiles:
                     here[s] = turned(s, j + 1)
@@ -262,9 +267,34 @@
                 curvature = curvature + value * change
                 low = face * value if low is None else low + face * value
                 high = before * value if high is None else high + before * value
-            ty[i, 0, :, c] = low
-            ty[i, 1, :, c] = high
+            ty[i, 0, piece, :] = low
+            ty[i, 1, piece, :] = high
         return curvature
+
+    sub = lax.broadcasted_iota(jnp.int32, (SUBLANES, LANES), 0)
+
+    def packed(get):
+        values = []
+        for g in range(row_tiles):
+            first = g * SUBLANES * SUBLANES
+            parts = [
+                get(pl.ds(first + k, SUBLANES, stride=SUBLANES)) for k in range(layers)
+            ]
+            while len(parts) > 1:
+                parts = [a + b for a, b in zip(parts[::2], parts[1::2])]
+            values.append(parts[0])
+        return values
+
+    def shifted(values, ahead):
+        turn, keep, whole = (
+            (LANES - 1, not_last, sub < SUBLANES - 1) if ahead else (1, not_first, sub > 0)
+        )
+        values = [pltpu.roll(v, turn, 1) for v in values]
+        moved = [pltpu.roll(v, SUBLANES - 1 if ahead else 1, 0) for v in values]
+        outside = moved[1:] + [0.0] if ahead else [0.0] + moved[:-1]
+        return [
+            jnp.where(keep, v, jnp.where(whole, m, o)) for v, m, o in zip(values, moved, outside)
+        ]
 
     def face_terms(f, low=True, high=True):
         for j in range(tiles):
@@ -279,47 +309,32 @@
                     difference = -adj[f + 1, s, :, c]
                 value = fx[f, s, :, c] * difference
                 total = value if total is None else total + value
-            txa[f, :, c] = total
-
-    sub = lax.broadcasted_iota(jnp.int32, (SUBLANES, LANES), 0)
-    below = [(sub // d) % 2 == 0 for d in (1, 2, 4)]
-
-    def fold(values):
-        for bit, d in enumerate((1, 2, 4)):
-            pairs = zip(values[::2], values[1::2])
-            values = [
-                jnp.where(below[bit], a, b) + pltpu.roll(jnp.where(below[bit], b, a), d, 0)
-                for a, b in pairs
-            ]
-        return values[0]
-
-    def folded(get):
-        return [
-            fold([get(cut(g * SUBLANES + k)) for k in range(SUBLANES)]) for g in range(row_tiles)
-        ]
+            txa[f, pl.ds(j * SUBLANES, SUBLANES), :] = total
+        for g, value in enumerate(packed(lambda rows_of: txa[f, rows_of, :])):
+            px[f, g] = value
 
     def pack_total(dst, first, i):
-        own = folded(
-            lambda c: txa[i, :, c] + txa[i + 1, :, c] + (ty[i, 0, :, c] - ty[i, 1, :, c])
-        )
-        low = [pltpu.roll(v, 1, 1) for v in folded(lambda c: ty[i, 0, :, c])]
-        high = [pltpu.roll(v, LANES - 1, 1) for v in folded(lambda c: ty[i, 1, :, c])]
-        zero = jnp.zeros((SUBLANES, LANES), F32)
-        low_down = [pltpu.roll(v, 1, 0) for v in low]
-        high_up = [pltpu.roll(v, SUBLANES - 1, 0) for v in high]
-        for g in range(row_tiles):
-            prior = low_down[g - 1] if g else zero
-            after = high_up[g + 1] if g + 1 < row_tiles else zero
-            from_low = jnp.where(not_first, low[g], jnp.where(sub > 0, low_down[g], prior))
-            from_high = jnp.where(
-                not_last, high[g], jnp.where(sub < SUBLANES - 1, high_up[g], after)
-            )
-            dst[first + g] = own[g] + from_low - from_high
+        low = packed(lambda rows_of: ty[i, 0, rows_of, :])
+        high = packed(lambda rows_of: ty[i, 1, rows_of, :])
+        term = [a - b for a, b in zip(low, shifted(high, True))]
+        for g, (a, b) in enumerate(zip(term, shifted(term, False))):
+            dst[first + g] = px[i, g] + px[i + 1, g] + (a + b)
 
     lax.fori_loop(1, rows, face_x, 0)
     loads["c"].wait()
     loads["w"].wait()
     curvature = lax.fori_loop(2, rows, cell_row, jnp.zeros((layers, LANES), F32))
+
+    near_tiles, far_tiles = range(tiles // 2), range(tiles // 2, tiles)
+    product = take(2)
+    arrived(pm.at[0, 0, :, :, near], halo + 1)
+    face_part(0, 0, near_tiles)
+    to_left, to_right = fx.at[0, 0, :, near], fx.at[last, 0, :, far]
+    send(to_left, fx.at[last, 0, :, near], (tm, left), product, product)
+    arrived(pm.at[last + 1, 0, :, :, far], halo)
+    face_part(last, 0, far_tiles)
+    send(to_right, fx.at[0, 0, :, far], (tm, right), product + 1, product + 1)
+    products = [started.pop(), started.pop()]
 
     def inner_faces(f, carry):
         face_terms(f)
@@ -343,17 +358,6 @@
         inner_pair,
         inner_pair,
     )
-
-    near_tiles, far_tiles = range(tiles // 2), range(tiles // 2, tiles)
-    product = take(2)
-    arrived(pm.at[0, 0, :, :, near], halo + 1)
-    face_part(0, 0, near_tiles)
-    to_left, to_right = fx.at[0, 0, :, near], fx.at[last, 0, :, far]
-    send(to_left, fx.at[last, 0, :, near], (tm, left), product, product)
-    arrived(pm.at[last + 1, 0, :, :, far], halo)
-    face_part(last, 0, far_tiles)
-    send(to_right, fx.at[0, 0, :, far], (tm, right), product + 1, product + 1)
-    products = [started.pop(), started.pop()]
 
     arrived(inner_in, inner_pair)
     inner_sum[...] = inner[pl.ds(core * half_tiles, half_tiles)] + inner_in[...]
@@ -377,21 +381,31 @@
         arrived(pm.at[0, s], halo + 2 * s + 1)
         face_part(0, s, range(tiles))
         face_part(last, s, range(tiles))
+
+    def no_face(states):
+        @pl.when(sp == 0)
+        def _():
+            for s in states:
+                fx[0, s] = jnp.zeros(wide, F32)
+
+        @pl.when(sp == spaces - 1)
+        def _():
+            for s in states:
+                fx[last, s] = jnp.zeros(wide, F32)
+
+    def edge_rows(states, add, curvature):
+        return lax.fori_loop(
+            0, 2, lambda k, carry: cell_row(1 + k * (rows - 1), carry, states, add), curvature
+        )
+
+    no_face(range(1, steps))
+    curvature = edge_rows(range(1, steps), False, curvature)
     arrived(fx.at[last, 0, :, near], product)
     arrived(fx.at[0, 0, :, far], product + 1)
-
     for copy in products:
         copy.wait_send()
-
-    @pl.when(sp == 0)
-    def _():
-        fx[0] = jnp.zeros((steps, layers, width), F32)
-
-    @pl.when(sp == spaces - 1)
-    def _():
-        fx[last] = jnp.zeros((steps, layers, width), F32)
-
-    curvature = lax.fori_loop(0, 2, lambda k, carry: cell_row(1 + k * (rows - 1), carry), curvature)
+    no_face(range(1))
+    curvature = edge_rows(range(1), True, curvature)
 
     sz[my_line] = jnp.sum(curvature, axis=0, keepdims=True)
     over_line = take(line)
@@ -405,8 +419,7 @@
     for c, (edge_row, inner_row, face) in enumerate(((0, 1, 0), (rows - 1, rows - 2, last))):
         pack_total(edges.at[c], 0, edge_row)
         pack_total(edges.at[c], row_tiles, inner_row)
-        for g, value in enumerate(folded(lambda k: txa[face, :, k])):
-            edges[c, 2 * row_tiles + g] = value
+        edges[c, pl.ds(2 * row_tiles, row_tiles)] = px[face]
     edge_pair = take(1)
     send(edges.at[1 - core], edges_in, (other, sp), edge_pair, edge_pair)
 
@@ -456,7 +469,8 @@
     def unpack(src, first, i):
         for j in range(tiles):
             low = j % SUBLANES
-            out[i : i + 1, cut(j)] = src[first + j // SUBLANES, low : low + 1, :]
+            value = src[first + j // SUBLANES, low : low + 1, :]
+            out[i : i + 1, cut(j)] = value * factor[i : i + 1, cut(j)]
 
     for k in range(1, zhs):
         whose = agb.at[core, pl.ds(((zh + zhs - k) % zhs) * chunk, chunk)]
@@ -521,7 +535,7 @@
     def block(*shape):
         return vmem((*shape, SUBLANES, LANES), F32)
 
-    total, curvature = pl.pallas_call(
+    product, curvature = pl.pallas_call(
         functools.partial(kernel, dims),
         out_shape=(
             jax.ShapeDtypeStruct((rows, width), F32),
@@ -542,11 +556,13 @@
             vmem((rows + 2, steps, 2, layers, width), F32),
             vmem((rows + 1, steps, layers, width), F32),
             vmem((rows + 2, steps, layers, width), F32),
-            vmem((rows + 1, layers, width), F32),
-            vmem((rows, 2, layers, width), F32),
+            vmem((rows + 1, tiles * layers, LANES), F32),
+            vmem((rows, 2, tiles * layers, LANES), F32),
             vmem((rows + 1, layers, width), F32),
             vmem((rows, layers, width), F32),
             vmem((rows, layers, width), F32),
+            vmem((rows, width), F32),
+            block(rows + 1, row_tiles),
             vmem((2, 1, width), F32),
             vmem((2, 1, width), F32),
             block(CORES * half_tiles),
@@ -581,8 +597,7 @@
         log_permeability,
         direction,
     )
-    factor = 0.25 / (layers * steps * tms)
-    return jnp.exp(log_permeability) * total * factor, curvature[0, 0]
+    return product, curvature[0, 0]
 
 
 def solution(mesh):

time: 42.6 us -> 42.8 us (level)
  other arithmetic: 1.59 us -> 0 us
  local copies, waits for them, and re-layouts: 0.01 us -> 1.57 us
    mul x1 -> x0, other arithmetic: 1.59 us -> none  [shards(): return (jnp.exp(log_permeability) * total * factor, curvature[0, 0])]
    unnamed x2 -> x1, local copies, waits for them, and re-layouts: 0.01 us -> 1.57 us
where the time goes in v4:
time: 42.8 us; the launch traced here: 42.6 us
  Pallas kernels  38.6 us (90%)
  between operations  2.45 us (6%)
  local copies, waits for them, and re-layouts  1.57 us (4%)
    pallas_call x1, Pallas kernels, shards(): pl.pallas_call(functools.partial(kernel, dims), out_shape=(jax.ShapeDtype...  38.6 us
    unnamed x1, local copies, waits for them, and re-layouts  1.57 us

profile of v4, /device:TPU:1, one launch (start us, length us, event | category | flops | bytes accessed | tf_op | source)
XLA Modules:
  0.0 42.6 jit_solution(16946848359403560594)
XLA Ops:
  0.6 38.6 %shard_map.77 = (f32[16,2048]{1,0:T(8,128)}, f32[1,128]{1,0:T(1,128)}) custom-call(f32[4096,128]{1,0:T(8,128)} %bitcast.22, f32[4096,128]{1,0:T(8,128)} %bitcast.23, f32[4096,128]{1,0:T(8,128)} %bitcast.24, f32[2048,128]{1,0:T(8,128)} %bitcast.25, f32[16,2048]{1,0:T(8,128)} %lp_hbm.1, f32[16,2048]{1,0:T(8,128)} %d_hbm.1), custom_call_target="tpu_custom_call" | custom-call | flops 26214400 | bytes 7340032 | tf_op jit(solution)/shard_map/pallas_call | solution.py:538
  39.3 1.6 %copy.10 = f32[16,2048]{1,0:T(8,128)} copy(f32[16,2048]{1,0:T(8,128)} %get-tuple-element.8) | data formatting | bytes 262144

commit v5 on v4

--- a/solution.py
+++ b/solution.py
@@ -41,7 +41,6 @@
     sby,
     sbb,
     factor,
-    px,
     sce,
     rce,
     inner,
@@ -100,20 +99,38 @@
     plane = ys * CHIPS_X
     my_plane = y * CHIPS_X + x
 
-    def line_peer(k):
-        index = (my_line + k) % line
-        to = index // CORES
-        return ((to // Z_LO) * CORES + index % CORES, sp - zl + to % Z_LO)
-
-    def plane_peer(k):
-        return (tm, ((my_plane + k) % plane) * Z_LO + zl)
+    def apart(k, n):
+        return min(k, n - k)
+
+    line_offsets = sorted(
+        ((dz, dc) for dz in range(zs) for dc in range(CORES) if (dz, dc) != (0, 0)),
+        key=lambda o: -apart(o[0], zs),
+    )
+    plane_offsets = sorted(
+        ((dy, dx) for dy in range(ys) for dx in range(CHIPS_X) if (dy, dx) != (0, 0)),
+        key=lambda o: -apart(o[0], ys) - apart(o[1], CHIPS_X),
+    )
+    z_offsets = sorted(range(1, zhs), key=lambda k: -apart(k, zhs))
+
+    def line_slot(dz, dc):
+        return ((z + dz + zs) % zs) * CORES + (core + dc + CORES) % CORES
+
+    def line_peer(dz, dc):
+        to = (z + dz) % zs
+        return ((to // Z_LO) * CORES + (core + dc) % CORES, sp - zl + to % Z_LO)
+
+    def plane_slot(dy, dx):
+        return ((y + dy + ys) % ys) * CHIPS_X + (x + dx + CHIPS_X) % CHIPS_X
+
+    def plane_peer(dy, dx):
+        return (tm, plane_slot(dy, dx) * Z_LO + zl)
 
     def z_peer(k):
         return (((zh + k) % zhs) * CORES + core, sp)
 
     greet = [(t, side) for side in (left, right) for t in range(tms)]
     greet += [((tm + k) % tms, sp) for k in range(1, tms)]
-    greet += [plane_peer(k) for k in range(1, plane)]
+    greet += [plane_peer(*o) for o in plane_offsets]
     barrier = pltpu.get_barrier_semaphore()
     for peer in greet:
         pl.semaphore_signal(barrier, inc=1, device_id=peer, device_id_type=MESH)
@@ -155,8 +172,15 @@
             for j in range(tiles):
                 pm[i + 1, s, which, :, cut(j)] = layers_of(ref, s, i, j)
 
-    near, far = pl.ds(0, width // 2), pl.ds(width // 2, width // 2)
+    def shares(s):
+        size = tiles // 2 if s == 0 else tiles // 4
+        return range(size), range(size, tiles - size), range(tiles - size, tiles)
+
+    def lanes_of(part):
+        return pl.ds(part[0] * LANES, len(part) * LANES)
+
     halo = take(2 * steps)
+    middle = take(2 * steps)
     for s in range(steps):
         loads["p", s].wait()
         loads["m", s].wait()
@@ -166,18 +190,19 @@
             load("c", c_hbm, cv, 2 * steps + 2)
             load("w", w_hbm, wv, 2 * steps + 3)
             pl.semaphore_wait(barrier, len(greet))
-        to_left, to_right = (far, near) if s == 0 else (pl.ds(0, width), pl.ds(0, width))
-        for row, goal, side, columns, index in (
-            (1, last + 1, left, to_left, halo + 2 * s),
-            (last, 0, right, to_right, halo + 2 * s + 1),
-        ):
-            send(
-                pm.at[row, s, :, :, columns],
-                pm.at[goal, s, :, :, columns],
-                (tm, side),
-                index,
-                index,
-            )
+        near, both, far = shares(s)
+        for first, parts in ((halo, (far, near)), (middle, (both, both))):
+            for k, part in enumerate(parts):
+                if len(part):
+                    row, goal, side = ((1, last + 1, left), (last, 0, right))[k]
+                    columns = lanes_of(part)
+                    send(
+                        pm.at[row, s, :, :, columns],
+                        pm.at[goal, s, :, :, columns],
+                        (tm, side),
+                        first + 2 * s + k,
+                        first + 2 * s + k,
+                    )
 
     loads["lp"].wait()
     loads["d"].wait()
@@ -271,30 +296,9 @@
             ty[i, 1, piece, :] = high
         return curvature
 
-    sub = lax.broadcasted_iota(jnp.int32, (SUBLANES, LANES), 0)
-
-    def packed(get):
-        values = []
-        for g in range(row_tiles):
-            first = g * SUBLANES * SUBLANES
-            parts = [
-                get(pl.ds(first + k, SUBLANES, stride=SUBLANES)) for k in range(layers)
-            ]
-            while len(parts) > 1:
-                parts = [a + b for a, b in zip(parts[::2], parts[1::2])]
-            values.append(parts[0])
-        return values
-
-    def shifted(values, ahead):
-        turn, keep, whole = (
-            (LANES - 1, not_last, sub < SUBLANES - 1) if ahead else (1, not_first, sub > 0)
-        )
-        values = [pltpu.roll(v, turn, 1) for v in values]
-        moved = [pltpu.roll(v, SUBLANES - 1 if ahead else 1, 0) for v in values]
-        outside = moved[1:] + [0.0] if ahead else [0.0] + moved[:-1]
-        return [
-            jnp.where(keep, v, jnp.where(whole, m, o)) for v, m, o in zip(values, moved, outside)
-        ]
+    def pack(dst, first, j, value):
+        low = j % SUBLANES
+        dst[first + j // SUBLANES, low : low + 1, :] = jnp.sum(value, axis=0, keepdims=True)
 
     def face_terms(f, low=True, high=True):
         for j in range(tiles):
@@ -310,37 +314,52 @@
                 value = fx[f, s, :, c] * difference
                 total = value if total is None else total + value
             txa[f, pl.ds(j * SUBLANES, SUBLANES), :] = total
-        for g, value in enumerate(packed(lambda rows_of: txa[f, rows_of, :])):
-            px[f, g] = value
+
+    def piece(j):
+        return pl.ds(j * SUBLANES, SUBLANES)
 
     def pack_total(dst, first, i):
-        low = packed(lambda rows_of: ty[i, 0, rows_of, :])
-        high = packed(lambda rows_of: ty[i, 1, rows_of, :])
-        term = [a - b for a, b in zip(low, shifted(high, True))]
-        for g, (a, b) in enumerate(zip(term, shifted(term, False))):
-            dst[first + g] = px[i, g] + px[i + 1, g] + (a + b)
+        high = [pltpu.roll(ty[i, 1, piece(j), :], LANES - 1, 1) for j in range(tiles)] + [0.0]
+        terms = [
+            ty[i, 0, piece(j), :] - jnp.where(not_last, high[j], high[j + 1])
+            for j in range(tiles)
+        ]
+        low = [0.0] + [pltpu.roll(v, 1, 1) for v in terms]
+        for j in range(tiles):
+            value = txa[i, piece(j), :] + txa[i + 1, piece(j), :]
+            value = value + (terms[j] + jnp.where(not_first, low[j + 1], low[j]))
+            pack(dst, first, j, value)
 
     lax.fori_loop(1, rows, face_x, 0)
     loads["c"].wait()
     loads["w"].wait()
     curvature = lax.fori_loop(2, rows, cell_row, jnp.zeros((layers, LANES), F32))
 
-    near_tiles, far_tiles = range(tiles // 2), range(tiles // 2, tiles)
-    product = take(2)
-    arrived(pm.at[0, 0, :, :, near], halo + 1)
-    face_part(0, 0, near_tiles)
-    to_left, to_right = fx.at[0, 0, :, near], fx.at[last, 0, :, far]
-    send(to_left, fx.at[last, 0, :, near], (tm, left), product, product)
-    arrived(pm.at[last + 1, 0, :, :, far], halo)
-    face_part(last, 0, far_tiles)
-    send(to_right, fx.at[0, 0, :, far], (tm, right), product + 1, product + 1)
-    products = [started.pop(), started.pop()]
+    product = take(2 * steps)
+    products = {}
+
+    def send_products(s):
+        near, _, far = shares(s)
+        for k, (f, goal, part, side, index) in enumerate(
+            ((0, last, near, left, halo + 1), (last, 0, far, right, halo))
+        ):
+            columns = lanes_of(part)
+            cells = 0 if f == 0 else last + 1
+            arrived(pm.at[cells, s, :, :, columns], index + 2 * s)
+            face_part(f, s, part)
+            number = product + 2 * s + k
+            send(fx.at[f, s, :, columns], fx.at[goal, s, :, columns], (tm, side), number, number)
+            products[s, k] = started.pop()
+
+    send_products(0)
 
     def inner_faces(f, carry):
         face_terms(f)
         return carry
 
     lax.fori_loop(2, rows - 1, inner_faces, 0)
+    for s in range(1, steps):
+        send_products(s)
 
     def inner_rows(i, carry):
         pack_total(inner, (i - 2) * row_tiles, i)
@@ -362,7 +381,7 @@
     arrived(inner_in, inner_pair)
     inner_sum[...] = inner[pl.ds(core * half_tiles, half_tiles)] + inner_in[...]
     scatter = take(zhs)
-    for k in range(1, zhs):
+    for k in z_offsets:
         to = (zh + k) % zhs
         send(
             inner_sum.at[pl.ds(to * chunk, chunk)],
@@ -376,11 +395,6 @@
     arrived(rce.at[1], edge)
     sbx[0] = jnp.broadcast_to(0.25 * (rce[0] + scaled[0:1, :]), wide)
     sbx[last] = jnp.broadcast_to(0.25 * (rce[1] + scaled[rows - 1 : rows, :]), wide)
-    for s in range(1, steps):
-        arrived(pm.at[last + 1, s], halo + 2 * s)
-        arrived(pm.at[0, s], halo + 2 * s + 1)
-        face_part(0, s, range(tiles))
-        face_part(last, s, range(tiles))
 
     def no_face(states):
         @pl.when(sp == 0)
@@ -398,19 +412,22 @@
             0, 2, lambda k, carry: cell_row(1 + k * (rows - 1), carry, states, add), curvature
         )
 
-    no_face(range(1, steps))
-    curvature = edge_rows(range(1, steps), False, curvature)
-    arrived(fx.at[last, 0, :, near], product)
-    arrived(fx.at[0, 0, :, far], product + 1)
-    for copy in products:
-        copy.wait_send()
-    no_face(range(1))
-    curvature = edge_rows(range(1), True, curvature)
+    for s in range(steps):
+        near, both, far = shares(s)
+        if len(both):
+            for f, cells, k in ((last, last + 1, 0), (0, 0, 1)):
+                arrived(pm.at[cells, s, :, :, lanes_of(both)], middle + 2 * s + k)
+                face_part(f, s, both)
+        for k, (f, part) in enumerate(((last, near), (0, far))):
+            arrived(fx.at[f, s, :, lanes_of(part)], product + 2 * s + k)
+            products[s, k].wait_send()
+        no_face((s,))
+        curvature = edge_rows((s,), s > 0, curvature)
 
     sz[my_line] = jnp.sum(curvature, axis=0, keepdims=True)
     over_line = take(line)
-    for k in range(1, line):
-        send(sz.at[my_line], sz.at[my_line], line_peer(k), over_line + k, over_line + k)
+    for k, o in enumerate(line_offsets):
+        send(sz.at[my_line], sz.at[my_line], line_peer(*o), over_line + k, over_line + k)
 
     face_terms(0, low=False)
     face_terms(last, high=False)
@@ -419,7 +436,8 @@
     for c, (edge_row, inner_row, face) in enumerate(((0, 1, 0), (rows - 1, rows - 2, last))):
         pack_total(edges.at[c], 0, edge_row)
         pack_total(edges.at[c], row_tiles, inner_row)
-        edges[c, pl.ds(2 * row_tiles, row_tiles)] = px[face]
+        for j in range(tiles):
+            pack(edges.at[c], 2 * row_tiles, j, txa[face, piece(j), :])
     edge_pair = take(1)
     send(edges.at[1 - core], edges_in, (other, sp), edge_pair, edge_pair)
 
@@ -431,7 +449,7 @@
     mine = agb.at[core, pl.ds(zh * chunk, chunk)]
     gather = take(zhs)
     forward = take(zhs)
-    for k in range(1, zhs):
+    for k in z_offsets:
         send(mine, mine, z_peer(k), gather + k, gather + k)
     send(mine, mine, (other, sp), forward, forward)
 
@@ -441,7 +459,7 @@
     edge_z[zh] = summed
     over_z = take(zhs)
     ghost = take(zhs)
-    for k in range(1, zhs):
+    for k in z_offsets:
         send(
             edge_z.at[zh, pl.ds(0, two)],
             edge_z.at[zh, pl.ds(0, two)],
@@ -450,7 +468,7 @@
             over_z + k,
         )
     side = left + core * (right - left)
-    for k in range(zhs):
+    for k in z_offsets + [0]:
         send(
             edge_z.at[zh, pl.ds(two, row_tiles)],
             ghost_z.at[zh],
@@ -459,12 +477,12 @@
             ghost + k,
         )
 
-    for k in range(1, line):
-        arrived(sz.at[(my_line + line - k) % line], over_line + k)
+    for k, (dz, dc) in enumerate(line_offsets):
+        arrived(sz.at[line_slot(-dz, -dc)], over_line + k)
     sxy[my_plane] = jnp.sum(sz[...], axis=0)
     over_plane = take(plane)
-    for k in range(1, plane):
-        send(sxy.at[my_plane], sxy.at[my_plane], plane_peer(k), over_plane + k, over_plane + k)
+    for k, o in enumerate(plane_offsets):
+        send(sxy.at[my_plane], sxy.at[my_plane], plane_peer(*o), over_plane + k, over_plane + k)
 
     def unpack(src, first, i):
         for j in range(tiles):
@@ -502,8 +520,8 @@
         unpack(final.at[c], 0, edge_row)
         unpack(final.at[c], row_tiles, inner_row)
 
-    for k in range(1, plane):
-        arrived(sxy.at[(my_plane + plane - k) % plane], over_plane + k)
+    for k, (dy, dx) in enumerate(plane_offsets):
+        arrived(sxy.at[plane_slot(-dy, -dx)], over_plane + k)
     whole = jnp.sum(sxy[...], axis=0)
     scale = 1.0 / (layers * steps * tms * rows * spaces * width)
     cur[...] = jnp.broadcast_to(jnp.sum(whole, axis=1, keepdims=True) * scale, cur.shape)
@@ -524,7 +542,7 @@
     row_tiles = tiles // SUBLANES
     half_tiles = (rows // CORES - 2) * row_tiles
     chunk = half_tiles // zhs
-    copies = 2 * steps + 4 + 3 + 5 * zhs + line + plane
+    copies = 6 * steps + 2 + 3 + 5 * zhs + line + plane
     vmem = pltpu.VMEM
 
     def in_tiles(array):
@@ -562,7 +580,6 @@
             vmem((rows, layers, width), F32),
             vmem((rows, layers, width), F32),
             vmem((rows, width), F32),
-            block(rows + 1, row_tiles),
             vmem((2, 1, width), F32),
             vmem((2, 1, width), F32),
             block(CORES * half_tiles),
@@ -582,7 +599,7 @@
             pltpu.SemaphoreType.DMA((copies,)),
         ],
         compiler_params=pltpu.CompilerParams(
-            collective_id=0, has_side_effects=True, vmem_limit_bytes=56 << 20
+            collective_id=0, has_side_effects=True, vmem_limit_bytes=55040 << 10
         ),
         cost_estimate=pl.CostEstimate(
             flops=50 * steps * flat * LANES,

time: 42.8 us -> 40 us (0.935)
  Pallas kernels: 38.6 us -> 37.5 us
  local copies, waits for them, and re-layouts: 1.57 us -> 0.66 us
  between operations: 2.45 us -> 1.8 us
    pallas_call x1, Pallas kernels: 38.6 us -> 37.5 us  [shards(): pl.pallas_call(functools.partial(kernel, dims), out_shape=(jax.ShapeDtype...]
    unnamed x1, local copies, waits for them, and re-layouts: 1.57 us -> 0.66 us
where the time goes in v5:
time: 40 us; the launch traced here: 39.9 us
  Pallas kernels  37.5 us (94%)
  between operations  1.8 us (4%)
  local copies, waits for them, and re-layouts  0.66 us (2%)
    pallas_call x1, Pallas kernels, shards(): pl.pallas_call(functools.partial(kernel, dims), out_shape=(jax.ShapeDtype...  37.5 us

profile of v5, /device:TPU:1, one launch (start us, length us, event | category | flops | bytes accessed | tf_op | source)
XLA Modules:
  0.0 39.9 jit_solution(3408652845747356110)
XLA Ops:
  0.6 37.5 %shard_map.77 = (f32[16,2048]{1,0:T(8,128)S(1)}, f32[1,128]{1,0:T(1,128)S(1)}) custom-call(f32[4096,128]{1,0:T(8,128)} %bitcast.23, f32[4096,128]{1,0:T(8,128)} %bitcast.24, f32[4096,128]{1,0:T(8,128)} %bitcast.25, f32[2048,128]{1,0:T(8,128)} %bitcast.26, f32[16,2048]{1,0:T(8,128)} %lp_hbm.1, f32[16,2048]{1,0:T(8,128)} %d_hbm.1), custom_call_target="tpu_custom_call" | custom-call | flops 26214400 | bytes 7340032 | tf_op jit(solution)/shard_map/pallas_call | solution.py:556
  38.1 0.7 %copy.10 = f32[16,2048]{1,0:T(8,128)} copy(f32[16,2048]{1,0:T(8,128)S(1)} %get-tuple-element.8) | data formatting | bytes 262144

commit v6 on v5

--- a/solution.py
+++ b/solution.py
@@ -87,13 +87,6 @@
         loads[name] = pltpu.make_async_copy(src, dst, local_sem.at[index])
         loads[name].start()
 
-    for s in range(steps):
-        part = pl.ds(s * state_rows, state_rows)
-        load(("p", s), p_hbm.at[part, :], pv.at[part, :], 2 * s)
-        load(("m", s), m_hbm.at[part, :], mv.at[part, :], 2 * s + 1)
-    load("lp", lp_hbm, lpv, 2 * steps)
-    load("d", d_hbm, dv, 2 * steps + 1)
-
     line = zs * CORES
     my_line = z * CORES + core
     plane = ys * CHIPS_X
@@ -128,12 +121,35 @@
     def z_peer(k):
         return (((zh + k) % zhs) * CORES + core, sp)
 
-    greet = [(t, side) for side in (left, right) for t in range(tms)]
-    greet += [((tm + k) % tms, sp) for k in range(1, tms)]
-    greet += [plane_peer(*o) for o in plane_offsets]
+    across = left + zl * (right - left)
+    greet = [(apart(dz, zs) + 0.5 * dc, line_peer(dz, dc)) for dz, dc in line_offsets]
+    greet += [
+        (apart(dy, ys) + apart(dx, CHIPS_X), plane_peer(dy, dx)) for dy, dx in plane_offsets
+    ]
+    greet += [
+        (
+            1.5 + Z_LO * apart(k, zhs),
+            (((zh + k) % zhs) * CORES + (core + c) % CORES, across),
+        )
+        for k in range(zhs)
+        for c in range(CORES)
+    ]
+    greet.sort(key=lambda entry: -entry[0])
     barrier = pltpu.get_barrier_semaphore()
-    for peer in greet:
-        pl.semaphore_signal(barrier, inc=1, device_id=peer, device_id_type=MESH)
+
+    def say(peers):
+        for _, peer in peers:
+            pl.semaphore_signal(barrier, inc=1, device_id=peer, device_id_type=MESH)
+
+    distant = sum(hops > 2.5 for hops, _ in greet)
+    say(greet[:distant])
+    for s in range(steps):
+        part = pl.ds(s * state_rows, state_rows)
+        load(("p", s), p_hbm.at[part, :], pv.at[part, :], 2 * s)
+        load(("m", s), m_hbm.at[part, :], mv.at[part, :], 2 * s + 1)
+    load("lp", lp_hbm, lpv, 2 * steps)
+    load("d", d_hbm, dv, 2 * steps + 1)
+    say(greet[distant:])
 
     sem_count = [0]
     started = []

time: 40 us -> 40 us (level)
  no operation moved by 1% of the time
where the time goes in v6:
time: 40 us; the launch traced here: 39.9 us
  Pallas kernels  37.5 us (94%)
  between operations  1.8 us (4%)
  local copies, waits for them, and re-layouts  0.66 us (2%)
    pallas_call x1, Pallas kernels, shards(): pl.pallas_call(functools.partial(kernel, dims), out_shape=(jax.ShapeDtype...  37.5 us

profile of v6, /device:TPU:1, one launch (start us, length us, event | category | flops | bytes accessed | tf_op | source)
XLA Modules:
  0.0 39.9 jit_solution(7939360616666899421)
XLA Ops:
  0.6 37.5 %shard_map.77 = (f32[16,2048]{1,0:T(8,128)S(1)}, f32[1,128]{1,0:T(1,128)S(1)}) custom-call(f32[4096,128]{1,0:T(8,128)} %bitcast.23, f32[4096,128]{1,0:T(8,128)} %bitcast.24, f32[4096,128]{1,0:T(8,128)} %bitcast.25, f32[2048,128]{1,0:T(8,128)} %bitcast.26, f32[16,2048]{1,0:T(8,128)} %lp_hbm.1, f32[16,2048]{1,0:T(8,128)} %d_hbm.1), custom_call_target="tpu_custom_call" | custom-call | flops 26214400 | bytes 7340032 | tf_op jit(solution)/shard_map/pallas_call | solution.py:572
  38.1 0.7 %copy.10 = f32[16,2048]{1,0:T(8,128)} copy(f32[16,2048]{1,0:T(8,128)S(1)} %get-tuple-element.8) | data formatting | bytes 262144

commit v7 on v6

--- a/solution.py
+++ b/solution.py
@@ -443,7 +443,7 @@
     sz[my_line] = jnp.sum(curvature, axis=0, keepdims=True)
     over_line = take(line)
     for k, o in enumerate(line_offsets):
-        send(sz.at[my_line], sz.at[my_line], line_peer(*o), over_line + k, over_line + k)
+        send(sz.at[my_line], sz.at[my_line], line_peer(*o), over_line + k, over_line)
 
     face_terms(0, low=False)
     face_terms(last, high=False)
@@ -493,12 +493,11 @@
             ghost + k,
         )
 
-    for k, (dz, dc) in enumerate(line_offsets):
-        arrived(sz.at[line_slot(-dz, -dc)], over_line + k)
+    arrived(sz.at[pl.ds(0, line - 1)], over_line)
     sxy[my_plane] = jnp.sum(sz[...], axis=0)
     over_plane = take(plane)
     for k, o in enumerate(plane_offsets):
-        send(sxy.at[my_plane], sxy.at[my_plane], plane_peer(*o), over_plane + k, over_plane + k)
+        send(sxy.at[my_plane], sxy.at[my_plane], plane_peer(*o), over_plane + k, over_plane)
 
     def unpack(src, first, i):
         for j in range(tiles):
@@ -536,14 +535,12 @@
         unpack(final.at[c], 0, edge_row)
         unpack(final.at[c], row_tiles, inner_row)
 
-    for k, (dy, dx) in enumerate(plane_offsets):
-        arrived(sxy.at[plane_slot(-dy, -dx)], over_plane + k)
+    for copy in started:
+        copy.wait_send()
+    arrived(sxy.at[pl.ds(0, plane - 1)], over_plane)
     whole = jnp.sum(sxy[...], axis=0)
     scale = 1.0 / (layers * steps * tms * rows * spaces * width)
     cur[...] = jnp.broadcast_to(jnp.sum(whole, axis=1, keepdims=True) * scale, cur.shape)
-
-    for copy in started:
-        copy.wait_send()
 
 
 def shards(tms, spaces, pressure, mobility, capacity, misfit_weight, log_permeability, direction):

time: 40 us -> 40 us (level)
  no operation moved by 1% of the time
where the time goes in v7:
time: 40 us; the launch traced here: 39.9 us
  Pallas kernels  37.5 us (94%)
  between operations  1.8 us (4%)
  local copies, waits for them, and re-layouts  0.66 us (2%)
    pallas_call x1, Pallas kernels, shards(): pl.pallas_call(functools.partial(kernel, dims), out_shape=(jax.ShapeDtype...  37.5 us

profile of v7, /device:TPU:1, one launch (start us, length us, event | category | flops | bytes accessed | tf_op | source)
XLA Modules:
  0.0 39.9 jit_solution(15900061192783862930)
XLA Ops:
  0.6 37.5 %shard_map.77 = (f32[16,2048]{1,0:T(8,128)S(1)}, f32[1,128]{1,0:T(1,128)S(1)}) custom-call(f32[4096,128]{1,0:T(8,128)} %bitcast.23, f32[4096,128]{1,0:T(8,128)} %bitcast.24, f32[4096,128]{1,0:T(8,128)} %bitcast.25, f32[2048,128]{1,0:T(8,128)} %bitcast.26, f32[16,2048]{1,0:T(8,128)} %lp_hbm.1, f32[16,2048]{1,0:T(8,128)} %d_hbm.1), custom_call_target="tpu_custom_call" | custom-call | flops 26214400 | bytes 7340032 | tf_op jit(solution)/shard_map/pallas_call | solution.py:569
  38.1 0.7 %copy.10 = f32[16,2048]{1,0:T(8,128)} copy(f32[16,2048]{1,0:T(8,128)S(1)} %get-tuple-element.8) | data formatting | bytes 262144

commit v8 on v7

--- a/solution.py
+++ b/solution.py
@@ -424,9 +424,9 @@
                 fx[last, s] = jnp.zeros(wide, F32)
 
     def edge_rows(states, add, curvature):
-        return lax.fori_loop(
-            0, 2, lambda k, carry: cell_row(1 + k * (rows - 1), carry, states, add), curvature
-        )
+        for r in (1, last):
+            curvature = cell_row(r, curvature, states, add)
+        return curvature
 
     for s in range(steps):
         near, both, far = shares(s)

time: 40 us -> 40 us (level)
  no operation moved by 1% of the time
where the time goes in v8:
time: 40 us; the launch traced here: 39.9 us
  Pallas kernels  37.5 us (94%)
  between operations  1.8 us (4%)
  local copies, waits for them, and re-layouts  0.66 us (2%)
    pallas_call x1, Pallas kernels, shards(): pl.pallas_call(functools.partial(kernel, dims), out_shape=(jax.ShapeDtype...  37.5 us

profile of v8, /device:TPU:1, one launch (start us, length us, event | category | flops | bytes accessed | tf_op | source)
XLA Modules:
  0.0 39.9 jit_solution(6715894665237103766)
XLA Ops:
  0.6 37.5 %shard_map.77 = (f32[16,2048]{1,0:T(8,128)S(1)}, f32[1,128]{1,0:T(1,128)S(1)}) custom-call(f32[4096,128]{1,0:T(8,128)} %bitcast.23, f32[4096,128]{1,0:T(8,128)} %bitcast.24, f32[4096,128]{1,0:T(8,128)} %bitcast.25, f32[2048,128]{1,0:T(8,128)} %bitcast.26, f32[16,2048]{1,0:T(8,128)} %lp_hbm.1, f32[16,2048]{1,0:T(8,128)} %d_hbm.1), custom_call_target="tpu_custom_call" | custom-call | flops 26214400 | bytes 7340032 | tf_op jit(solution)/shard_map/pallas_call | solution.py:569
  38.1 0.7 %copy.10 = f32[16,2048]{1,0:T(8,128)} copy(f32[16,2048]{1,0:T(8,128)S(1)} %get-tuple-element.8) | data formatting | bytes 262144

commit v9 on v7

--- a/solution.py
+++ b/solution.py
@@ -394,6 +394,44 @@
         inner_pair,
     )
 
+    arrived(rce.at[0], edge + 1)
+    arrived(rce.at[1], edge)
+    sbx[0] = jnp.broadcast_to(0.25 * (rce[0] + scaled[0:1, :]), wide)
+    sbx[last] = jnp.broadcast_to(0.25 * (rce[1] + scaled[rows - 1 : rows, :]), wide)
+
+    def no_face(states):
+        @pl.when(sp == 0)
+        def _():
+            for s in states:
+                fx[0, s] = jnp.zeros(wide, F32)
+
+        @pl.when(sp == spaces - 1)
+        def _():
+            for s in states:
+                fx[last, s] = jnp.zeros(wide, F32)
+
+    def edge_rows(states, add, curvature):
+        return lax.fori_loop(
+            0, 2, lambda k, carry: cell_row(1 + k * (rows - 1), carry, states, add), curvature
+        )
+
+    for s in range(steps):
+        near, both, far = shares(s)
+        if len(both):
+            for f, cells, k in ((last, last + 1, 0), (0, 0, 1)):
+                arrived(pm.at[cells, s, :, :, lanes_of(both)], middle + 2 * s + k)
+                face_part(f, s, both)
+        for k, (f, part) in enumerate(((last, near), (0, far))):
+            arrived(fx.at[f, s, :, lanes_of(part)], product + 2 * s + k)
+            products[s, k].wait_send()
+        no_face((s,))
+        curvature = edge_rows((s,), s > 0, curvature)
+
+    sz[my_line] = jnp.sum(curvature, axis=0, keepdims=True)
+    over_line = take(line)
+    for k, o in enumerate(line_offsets):
+        send(sz.at[my_line], sz.at[my_line], line_peer(*o), over_line + k, over_line)
+
     arrived(inner_in, inner_pair)
     inner_sum[...] = inner[pl.ds(core * half_tiles, half_tiles)] + inner_in[...]
     scatter = take(zhs)
@@ -407,44 +445,6 @@
             scatter + k,
         )
 
-    arrived(rce.at[0], edge + 1)
-    arrived(rce.at[1], edge)
-    sbx[0] = jnp.broadcast_to(0.25 * (rce[0] + scaled[0:1, :]), wide)
-    sbx[last] = jnp.broadcast_to(0.25 * (rce[1] + scaled[rows - 1 : rows, :]), wide)
-
-    def no_face(states):
-        @pl.when(sp == 0)
-        def _():
-            for s in states:
-                fx[0, s] = jnp.zeros(wide, F32)
-
-        @pl.when(sp == spaces - 1)
-        def _():
-            for s in states:
-                fx[last, s] = jnp.zeros(wide, F32)
-
-    def edge_rows(states, add, curvature):
-        return lax.fori_loop(
-            0, 2, lambda k, carry: cell_row(1 + k * (rows - 1), carry, states, add), curvature
-        )
-
-    for s in range(steps):
-        near, both, far = shares(s)
-        if len(both):
-            for f, cells, k in ((last, last + 1, 0), (0, 0, 1)):
-                arrived(pm.at[cells, s, :, :, lanes_of(both)], middle + 2 * s + k)
-                face_part(f, s, both)
-        for k, (f, part) in enumerate(((last, near), (0, far))):
-            arrived(fx.at[f, s, :, lanes_of(part)], product + 2 * s + k)
-            products[s, k].wait_send()
-        no_face((s,))
-        curvature = edge_rows((s,), s > 0, curvature)
-
-    sz[my_line] = jnp.sum(curvature, axis=0, keepdims=True)
-    over_line = take(line)
-    for k, o in enumerate(line_offsets):
-        send(sz.at[my_line], sz.at[my_line], line_peer(*o), over_line + k, over_line)
-
     face_terms(0, low=False)
     face_terms(last, high=False)
     face_terms(1)
@@ -456,18 +456,6 @@
             pack(edges.at[c], 2 * row_tiles, j, txa[face, piece(j), :])
     edge_pair = take(1)
     send(edges.at[1 - core], edges_in, (other, sp), edge_pair, edge_pair)
-
-    reduced = inner_sum[pl.ds(zh * chunk, chunk)]
-    for k in range(1, zhs):
-        arrived(rsb.at[k], scatter + k)
-        reduced = reduced + rsb[k]
-    agb[core, pl.ds(zh * chunk, chunk)] = reduced
-    mine = agb.at[core, pl.ds(zh * chunk, chunk)]
-    gather = take(zhs)
-    forward = take(zhs)
-    for k in z_offsets:
-        send(mine, mine, z_peer(k), gather + k, gather + k)
-    send(mine, mine, (other, sp), forward, forward)
 
     two = 2 * row_tiles
     arrived(edges_in, edge_pair)
@@ -492,6 +480,18 @@
             ghost + k,
             ghost + k,
         )
+
+    reduced = inner_sum[pl.ds(zh * chunk, chunk)]
+    for k in range(1, zhs):
+        arrived(rsb.at[k], scatter + k)
+        reduced = reduced + rsb[k]
+    agb[core, pl.ds(zh * chunk, chunk)] = reduced
+    mine = agb.at[core, pl.ds(zh * chunk, chunk)]
+    gather = take(zhs)
+    forward = take(zhs)
+    for k in z_offsets:
+        send(mine, mine, z_peer(k), gather + k, gather + k)
+    send(mine, mine, (other, sp), forward, forward)
 
     arrived(sz.at[pl.ds(0, line - 1)], over_line)
     sxy[my_plane] = jnp.sum(sz[...], axis=0)

time: 40 us -> 40.8 us (1.020)
  Pallas kernels: 37.5 us -> 38.3 us
    pallas_call x1, Pallas kernels: 37.5 us -> 38.3 us  [shards(): pl.pallas_call(functools.partial(kernel, dims), out_shape=(jax.ShapeDtype...]
where the time goes in v9:
time: 40.8 us; the launch traced here: 40.7 us
  Pallas kernels  38.3 us (94%)
  between operations  1.8 us (4%)
  local copies, waits for them, and re-layouts  0.66 us (2%)
    pallas_call x1, Pallas kernels, shards(): pl.pallas_call(functools.partial(kernel, dims), out_shape=(jax.ShapeDtype...  38.3 us

profile of v9, /device:TPU:1, one launch (start us, length us, event | category | flops | bytes accessed | tf_op | source)
XLA Modules:
  0.0 40.7 jit_solution(16984380503885816105)
XLA Ops:
  0.6 38.3 %shard_map.77 = (f32[16,2048]{1,0:T(8,128)S(1)}, f32[1,128]{1,0:T(1,128)S(1)}) custom-call(f32[4096,128]{1,0:T(8,128)} %bitcast.23, f32[4096,128]{1,0:T(8,128)} %bitcast.24, f32[4096,128]{1,0:T(8,128)} %bitcast.25, f32[2048,128]{1,0:T(8,128)} %bitcast.26, f32[16,2048]{1,0:T(8,128)} %lp_hbm.1, f32[16,2048]{1,0:T(8,128)} %d_hbm.1), custom_call_target="tpu_custom_call" | custom-call | flops 26214400 | bytes 7340032 | tf_op jit(solution)/shard_map/pallas_call | solution.py:569
  38.9 0.7 %copy.10 = f32[16,2048]{1,0:T(8,128)} copy(f32[16,2048]{1,0:T(8,128)S(1)} %get-tuple-element.8) | data formatting | bytes 262144

commit v10 on v7

--- a/solution.py
+++ b/solution.py
@@ -367,15 +367,14 @@
             send(fx.at[f, s, :, columns], fx.at[goal, s, :, columns], (tm, side), number, number)
             products[s, k] = started.pop()
 
-    send_products(0)
+    for s in range(steps):
+        send_products(s)
 
     def inner_faces(f, carry):
         face_terms(f)
         return carry
 
     lax.fori_loop(2, rows - 1, inner_faces, 0)
-    for s in range(1, steps):
-        send_products(s)
 
     def inner_rows(i, carry):
         pack_total(inner, (i - 2) * row_tiles, i)

time: 40 us -> 39.9 us (level)
  no operation moved by 1% of the time
where the time goes in v10:
time: 39.9 us; the launch traced here: 39.8 us
  Pallas kernels  37.3 us (93%)
  between operations  1.8 us (5%)
  local copies, waits for them, and re-layouts  0.66 us (2%)
    pallas_call x1, Pallas kernels, shards(): pl.pallas_call(functools.partial(kernel, dims), out_shape=(jax.ShapeDtype...  37.3 us

profile of v10, /device:TPU:1, one launch (start us, length us, event | category | flops | bytes accessed | tf_op | source)
XLA Modules:
  0.0 39.8 jit_solution(8685303245191356359)
XLA Ops:
  0.6 37.3 %shard_map.77 = (f32[16,2048]{1,0:T(8,128)S(1)}, f32[1,128]{1,0:T(1,128)S(1)}) custom-call(f32[4096,128]{1,0:T(8,128)} %bitcast.23, f32[4096,128]{1,0:T(8,128)} %bitcast.24, f32[4096,128]{1,0:T(8,128)} %bitcast.25, f32[2048,128]{1,0:T(8,128)} %bitcast.26, f32[16,2048]{1,0:T(8,128)} %lp_hbm.1, f32[16,2048]{1,0:T(8,128)} %d_hbm.1), custom_call_target="tpu_custom_call" | custom-call | flops 26214400 | bytes 7340032 | tf_op jit(solution)/shard_map/pallas_call | solution.py:568
  38.0 0.7 %copy.10 = f32[16,2048]{1,0:T(8,128)} copy(f32[16,2048]{1,0:T(8,128)S(1)} %get-tuple-element.8) | data formatting | bytes 262144
